TPU v7x, 128 devices: a whole 4x4x4 slice. The times are simulated.
128 devices in a mesh: comp: 8 (over x, core), blk: 16 (over y, z).
Axes of the slice: x: 4, y: 4, z: 4, core: 2. Of those that a mesh axis runs over, the one named last changes fastest.
Arguments:
- start_modes: float32 [8, 65536, 256], P('comp', 'blk')
- stiff_diag: float32 [8, 512, 128, 128], P('comp', 'blk')
- stiff_off: float32 [8, 512, 128, 128], P('comp', 'blk'), may hold values from -0.625 to 0.625
- mass_blocks: float32 [8, 512, 128, 128], P('comp', 'blk')
- coupling: float32 [8, 512, 128, 128], P('comp', 'blk'), may hold values from -6 to 6
- interface_block: int32 [8, 512], P('comp', 'blk'), may hold values from 0 to 16
- global_iface: int32 [8, 16], P('comp'), may hold values from 0 to 31
Outputs:
- modes: float32 [8, 65536, 256], P('comp', 'blk')
- reduced_stiffness: float32 [8, 256, 256], P('comp')
- assembled: float32 [32, 128, 128], P('comp')
All inputs are finite; a program needn't handle non-finite values.
Results may differ from a plain program's by a relative error of at most 0.0003.
Values sent between devices are 32-bit elements; how exact they have to be, the bound alone decides.
A program may use at most 128 MiB of HBM per device.

v0:
```python
import jax
import jax.numpy as jnp
from jax import lax
from jax.sharding import PartitionSpec as P

ITERS = 2
GIFC = 4


highest = lax.Precision.HIGHEST
step_size = 0.15


def passed_along(value, axis, steps):
    count = lax.axis_size(axis)
    initial, last = (max(0, -steps), min(count, count - steps))
    return lax.ppermute(value, axis, [(source, source + steps) for source in range(initial, last)])


def extended_2(block, sides, width):
    for axis, dim in sides:
        count = lax.axis_size(axis)
        forward = [(i, i + 1) for i in range(count - 1)]
        backward = [(target, source) for source, target in forward]
        low = lax.ppermute(
            lax.slice_in_dim(block, block.shape[dim] - width, None, axis=dim), axis, forward
        )
        high = lax.ppermute(lax.slice_in_dim(block, 0, width, axis=dim), axis, backward)
        block = jnp.concatenate([low, block, high], axis=dim)
    return block


def rows_for(lines, peers):
    spare = -len(lines) % peers
    return jnp.pad(lines, [(0, spare)] + [(0, 0)] * (lines.ndim - 1))


def copy_for_each(array, axis):
    copies = jnp.broadcast_to(array, (lax.axis_size(axis), *array.shape))
    return lax.all_to_all(copies, axis, split_axis=0, concat_axis=0, tiled=True)


def in_order(pieces, dim):
    dims = list(pieces.shape[1:])
    dims[dim] *= pieces.shape[0]
    return jnp.moveaxis(pieces, 0, dim).reshape(dims)


def collect(array, axis, dim):
    pieces = copy_for_each(array, axis)
    return in_order(pieces, dim)


def split_up(array, dim, peers):
    dims = array.shape
    pieces = array.reshape(*dims[:dim], peers, dims[dim] // peers, *dims[dim + 1 :])
    return jnp.moveaxis(pieces, dim, 0)


def sent_and_summed(array, axis, dim):
    peers = lax.axis_size(axis)
    pieces = lax.all_to_all(split_up(array, dim, peers), axis, 0, 0, tiled=True)
    return jnp.sum(pieces, axis=0)


def sum_by_parts(array, axes):
    padded = rows_for(array, lax.axis_size(axes))
    whole = collect(sent_and_summed(padded, axes, 0), axes, 0)
    return lax.slice_in_dim(whole, 0, len(array)).reshape(array.shape)


def in_one(arrays, axis):
    line, at, gathered = (jnp.concatenate([a.reshape(-1) for a in arrays]), 0, [])
    subtotal = sum_by_parts(line, axis)
    for a in arrays:
        gathered.append(subtotal[at : at + a.size].reshape(a.shape))
        at += a.size
    return tuple(gathered)


def total_of(array, axes):
    lines = array.reshape(-1, array.shape[-1])
    own = sent_and_summed(rows_for(lines, lax.axis_size(axes)), axes, 0)
    whole = collect(own, axes, 0)
    return whole[: len(lines)].reshape(array.shape)


def block_product(blocks, vectors):
    return jnp.einsum("bij,bjm->bim", blocks, vectors, precision=highest)


def lower_inverse(matrix):
    factor = jnp.linalg.cholesky(matrix)
    unit_matrix = jnp.eye(matrix.shape[0], dtype=matrix.dtype)
    return lax.linalg.triangular_solve(factor, unit_matrix, left_side=True, lower=True)


def local(start_modes, stiff_diag, stiff_off, mass_blocks, coupling, interface_block, global_iface):
    start_flat = start_modes[0]
    stiff_self = stiff_diag[0]
    stiff_link = stiff_off[0]
    mass_self = mass_blocks[0]
    coupling_blocks = coupling[0]
    interface_ids = interface_block[0]
    global_ids = global_iface[0]
    row_count, mode_count = start_flat.shape
    blocks_dev = stiff_self.shape[0]
    block_size = stiff_self.shape[1]
    dof_count = row_count * lax.axis_size("blk")
    link_next = passed_along(stiff_link[:1], "blk", -1)
    link_after = jnp.concatenate([stiff_link[1:], link_next], 0)

    def stiff_apply(vectors):
        padded = extended_2(vectors, (("blk", 0),), block_size)
        extended = padded.reshape(blocks_dev + 2, block_size, mode_count)
        result = block_product(stiff_self, extended[1 : blocks_dev + 1]) + block_product(
            stiff_link, extended[:blocks_dev]
        )
        result = result + jnp.einsum("bji,bjm->bim", link_after, extended[2:], precision=highest)
        return result.reshape(row_count, mode_count)

    def gram_matrix(left, right):
        return jnp.dot(left.T, right, precision=highest) / dof_count

    basis = start_flat
    stiff_basis = stiff_apply(basis)
    reduced = jnp.zeros((mode_count, mode_count), jnp.float32)
    for sweep in range(ITERS):
        filtered = basis - step_size * stiff_basis
        mass_part = block_product(
            mass_self, filtered.reshape(blocks_dev, block_size, mode_count)
        ).reshape(row_count, mode_count)
        stiff_part = stiff_apply(filtered)
        mass_gram, stiff_gram = in_one(
            (gram_matrix(filtered, mass_part), gram_matrix(filtered, stiff_part)), "blk"
        )
        factor_inv = lower_inverse(mass_gram)
        basis = jnp.dot(filtered, factor_inv.T, precision=highest)
        if sweep + 1 < ITERS:
            stiff_basis = jnp.dot(stiff_part, factor_inv.T, precision=highest)
        reduced = jnp.dot(
            jnp.dot(factor_inv, stiff_gram, precision=highest), factor_inv.T, precision=highest
        )
    iface_count = global_ids.shape[0]
    block_terms = jnp.einsum(
        "bkm,bkl->bml",
        basis.reshape(blocks_dev, block_size, mode_count),
        coupling_blocks,
        precision=highest,
    )
    onehot = (interface_ids[:, None] == jnp.arange(iface_count, dtype=jnp.int32)[None, :]).astype(
        jnp.float32
    )
    coupling_term = (
        jnp.einsum("bj,bml->mjl", onehot, block_terms, precision=highest) / dof_count**0.5
    )
    reduced_inv = lower_inverse(reduced)
    shared = total_of(coupling_term, "blk")
    scaled = jnp.einsum("nm,mjl->njl", reduced_inv, shared, precision=highest)
    condensed = jnp.einsum("njk,njl->jkl", scaled, scaled, precision=highest)
    global_count = GIFC * lax.axis_size("comp")
    placed = (global_ids[:, None] == jnp.arange(global_count, dtype=jnp.int32)[None, :]).astype(
        jnp.float32
    )
    dense_sum = jnp.einsum("jg,jkl->gkl", placed, condensed, precision=highest)
    owned = sent_and_summed(dense_sum, "comp", 0)
    return (basis[None], reduced[None], owned)


def solution(mesh):
    in_specs = (
        P("comp", "blk", None),
        P("comp", "blk", None, None),
        P("comp", "blk", None, None),
        P("comp", "blk", None, None),
        P("comp", "blk", None, None),
        P("comp", "blk"),
        P("comp", None),
    )
    out_specs = (P("comp", "blk", None), P("comp", None, None), P("comp", None, None))
    return jax.shard_map(local, mesh=mesh, in_specs=in_specs, out_specs=out_specs, check_vma=False)
```

profile of v0, /device:TPU:1, one launch (start us, length us, event | category | flops | bytes accessed | tf_op | source)
XLA Modules:
  0.0 478.0 jit_solution(3618256241685834553)
XLA Ops:
  1.8 4.4 collective-permute-start
  9.7 8.2 %fusion.25 = f32[32,128,256]{2,1,0:T(8,128)} fusion(f32[32,128,256]{2,1,0:T(8,128)} %bitcast.207, f32[1,32,128,128]{3,2,1,0:T(8,128)S(1)} %copy-done), kind=kOutput, calls=%fused_computation.44 | convolution fusion | flops 1610612736 | bytes 10485760 | tf_op jit(solution)/shard_map/bij,bjm->bim/dot_general | solution.py:89
  17.9 1.5 slice.144
  19.4 3.4 copy.48
  22.8 4.1 pad_maximum_fusion.4
  26.9 5.3 %fusion.19 = f32[32,256,128]{1,2,0:T(8,128)} fusion(f32[32,128,256]{2,1,0:T(8,128)S(1)} %bitcast.217, f32[1,32,128,128]{3,2,1,0:T(8,128)S(1)} %copy-done.10), kind=kOutput, calls=%fused_computation.38 | convolution fusion | flops 1610612736 | bytes 10485760 | tf_op jit(solution)/shard_map/bij,bjm->bim/dot_general | solution.py:89
  32.2 6.6 %fusion.6 = f32[32,128,256]{2,1,0:T(8,128)S(1)} fusion(f32[32,128,256]{2,1,0:T(8,128)} %fusion.25, f32[32,256,128]{1,2,0:T(8,128)} %fusion.19, f32[32,128,256]{2,1,0:T(8,128)S(1)} %bitcast.223, f32[1,128,128]{1,2,0:T(8,128)S(1)} %collective-permute-done.1, f32[31,128,128]{1,2,0:T(8,128)S(1)} %bitcast.214), kind=kOutput, calls=%fused_computation.24 | convolution fusion | flops 1614282752 | bytes 18874368 | tf_op jit(solution)/shard_map/bji,bjm->bim/dot_general | solution.py:119
  39.7 5.4 %fusion.23 = f32[32,256,128]{1,2,0:T(8,128)} fusion(f32[1,32,128,128]{3,2,1,0:T(8,128)S(1)} %copy-done, f32[32,128,256]{2,1,0:T(8,128)S(1)} %bitcast.209, f32[32,128,256]{2,1,0:T(8,128)S(1)} %fusion.6), kind=kOutput, calls=%fused_computation.42 | convolution fusion | flops 1611661312 | bytes 14680064 | tf_op jit(solution)/shard_map/bij,bjm->bim/dot_general | solution.py:89
  45.1 4.8 %collective-permute-start.3 = (f32[128,256]{1,0:T(8,128)S(1)}, f32[128,256]{1,0:T(8,128)S(1)}, u32[]{:S(2)}, u32[]{:S(2)}) collective-permute-start(f32[128,256]{1,0:T(8,128)S(1)} %get-tuple-element.73), channel_id=1, source_target_pairs={{0,1},{1,2},{2,3},{3,4},{4,5},{5,6},{6,7},{7,8},{8,9},{9,10},{10,1... | collective-permute-start | bytes 393224 | tf_op jit(solution)/shard_map/ppermute | solution.py:25
  49.9 1.5 collective-permute-start.4
  53.0 4.2 fusion.13
  57.2 6.8 %fusion.34 = f32[256,256]{1,0:T(8,128)S(1)} fusion(f32[4096,256]{1,0:T(8,128)S(1)} %bitcast.220, f32[1,4096,256]{2,1,0:T(8,128)S(1)} %bitcast_subtract_fusion), kind=kOutput, calls=%fused_computation.51 | convolution fusion | flops 3221291008 | bytes 8650752 | tf_op jit(solution)/shard_map/dot_general | solution.py:123
  64.0 4.5 pad_maximum_fusion.2
  68.5 5.3 %fusion.17 = f32[32,256,128]{1,2,0:T(8,128)} fusion(f32[32,128,256]{2,1,0:T(8,128)S(1)} %bitcast.218, f32[1,32,128,128]{3,2,1,0:T(8,128)S(1)} %copy-done.11), kind=kOutput, calls=%fused_computation.36 | convolution fusion | flops 1610612736 | bytes 10485760 | tf_op jit(solution)/shard_map/bij,bjm->bim/dot_general | solution.py:89
  73.8 6.2 %bitcast_add_fusion.1 = f32[32,128,256]{2,1,0:T(8,128)S(1)} fusion(f32[32,256,128]{1,2,0:T(8,128)S(1)} %copy-done.17, f32[32,256,128]{1,2,0:T(8,128)} %fusion.17, f32[32,128,256]{2,1,0:T(8,128)S(1)} %bitcast.226, f32[1,128,128]{1,2,0:T(8,128)S(1)} %collective-permute-done.1, f32[31,128,128]{1,2,0:T(8,128)S(1)} %bitcast.215), kind=kOutput, calls=%fused_computation.15 | convolution fusion | flops 1613234176 | bytes 18874368 | tf_op jit(solution)/shard_map/bji,bjm->bim/dot_general | solution.py:119
  80.1 1.9 copy-done.7
  82.0 7.1 %fusion.37 = f32[256,256]{1,0:T(8,128)S(1)} fusion(f32[4096,256]{1,0:T(8,128)S(1)} %bitcast.212, f32[1,4096,256]{2,1,0:T(8,128)S(1)} %copy-done.6), kind=kOutput, calls=%fused_computation.52 | convolution fusion | flops 3221291008 | bytes 8650752 | tf_op jit(solution)/shard_map/dot_general | solution.py:123
  90.6 10.4 %all-to-all-start = ((f32[16,1,8192]{2,1,0:T(1,128)}), f32[16,1,8192]{2,1,0:T(1,128)S(1)}, u32[]{:S(2)}, u32[]{:S(2)}) async-start(f32[16,1,8192]{2,1,0:T(1,128)} %all_to_all.29), calls=%async_computation | async-start | bytes 1048576 | tf_op jit(solution)/shard_map/all_to_all | solution.py:62
  101.0 9.2 %all-to-all-done = f32[16,1,8192]{2,1,0:T(1,128)S(1)} async-done(((f32[16,1,8192]{2,1,0:T(1,128)}), f32[16,1,8192]{2,1,0:T(1,128)S(1)}, u32[]{:S(2)}, u32[]{:S(2)}) %all-to-all-start) | async-done | bytes 524320 | tf_op jit(solution)/shard_map/all_to_all | solution.py:62
  111.7 3.6 all-to-all-start.1
  115.4 8.9 %all-to-all-done.1 = f32[16,1,8192]{2,1,0:T(1,128)S(1)} async-done(((f32[16,1,8192]{2,1,0:T(1,128)}), f32[16,1,8192]{2,1,0:T(1,128)S(1)}, u32[]{:S(2)}, u32[]{:S(2)}) %all-to-all-start.1) | async-done | bytes 524320 | tf_op jit(solution)/shard_map/all_to_all | solution.py:40
  125.1 11.7 %cholesky.172 = f32[128,128]{1,0:T(8,128)S(1)} custom-call(f32[128,128]{1,0:T(8,128)S(1)} %cholesky.270), custom_call_target="Cholesky" | custom-call | tf_op jit(solution)/shard_map/jit(cholesky)/cholesky | solution.py:93
  136.9 9.8 %custom-call.15 = f32[1,128,128]{1,2,0:T(8,128)S(1)} custom-call(f32[1,128,128]{2,1,0:T(8,128)S(1)} %get-tuple-element.89), custom_call_target="InvertDiagBlocksLowerTriangular" | custom-call | tf_op jit(solution)/shard_map/jit(cholesky)/cholesky | solution.py:93
  147.2 11.7 %cholesky.189 = f32[128,128]{1,0:T(8,128)S(1)} custom-call(f32[128,128]{1,0:T(8,128)S(1)} %convolution_subtract_fusion.5), custom_call_target="Cholesky" | custom-call | tf_op jit(solution)/shard_map/jit(cholesky)/cholesky | solution.py:93
  160.9 3.8 while.6
  164.7 19.9 %custom-call.16 = f32[2,128,128]{1,2,0:T(8,128)S(1)} custom-call(f32[2,128,128]{2,1,0:T(8,128)S(1)} %get-tuple-element.25), custom_call_target="InvertDiagBlocksLowerTriangular" | custom-call | tf_op jit(solution)/shard_map/triangular_solve/custom-call.0 | solution.py:95
  185.5 5.6 %fusion.48 = f32[4096,256]{1,0:T(8,128)S(1)} fusion(f32[4096,256]{1,0:T(8,128)} %copy-done.4, f32[128,256]{1,0:T(8,128)S(1)} %fusion.67, f32[128,256]{1,0:T(8,128)S(1)} %fusion.56), kind=kOutput, calls=%fused_computation.85 | convolution fusion | flops 3221291008 | bytes 8650752 | tf_op jit(solution)/shard_map/dot_general | solution.py:138
  191.2 3.6 fusion
  194.8 4.6 fusion.11
  199.4 5.3 %fusion.21 = f32[32,256,128]{1,2,0:T(8,128)} fusion(f32[32,128,256]{2,1,0:T(8,128)S(1)} %bitcast.206, f32[1,32,128,128]{3,2,1,0:T(8,128)S(1)} %copy-done), kind=kOutput, calls=%fused_computation.40 | convolution fusion | flops 1610612736 | bytes 10485760 | tf_op jit(solution)/shard_map/bij,bjm->bim/dot_general | solution.py:89
  204.7 2.2 collective-permute-start.5
  206.9 1.7 collective-permute-start.6
  208.7 7.1 %convolution_multiply_fusion.2 = f32[256,256]{1,0:T(8,128)S(1)} fusion(f32[4096,256]{1,0:T(8,128)S(1)} %fusion, f32[4096,256]{1,0:T(8,128)S(1)} %bitcast.224), kind=kOutput, calls=%fused_computation.54 | convolution fusion | flops 3221291008 | bytes 8650752 | tf_op jit(solution)/shard_map/dot_general | solution.py:123
  215.8 4.1 pad_maximum_fusion
  219.9 5.5 %fusion.15 = f32[32,256,128]{1,2,0:T(8,128)} fusion(f32[32,128,256]{2,1,0:T(8,128)S(1)} %bitcast.219, f32[1,32,128,128]{3,2,1,0:T(8,128)S(1)} %copy-done.12), kind=kOutput, calls=%fused_computation.34 | convolution fusion | flops 1610612736 | bytes 10485760 | tf_op jit(solution)/shard_map/bij,bjm->bim/dot_general | solution.py:89
  225.4 6.2 %bitcast_add_fusion = f32[32,128,256]{2,1,0:T(8,128)S(1)} fusion(f32[32,256,128]{1,2,0:T(8,128)S(1)} %copy-done.18, f32[32,256,128]{1,2,0:T(8,128)} %fusion.15, f32[32,128,256]{2,1,0:T(8,128)S(1)} %bitcast.225, f32[1,128,128]{1,2,0:T(8,128)S(1)} %collective-permute-done.1, f32[31,128,128]{1,2,0:T(8,128)S(1)} %bitcast.216), kind=kOutput, calls=%fused_computation.14 | convolution fusion | flops 1613234176 | bytes 18874368 | tf_op jit(solution)/shard_map/bji,bjm->bim/dot_general | solution.py:119
  231.6 7.0 %convolution_multiply_fusion.1 = f32[256,256]{1,0:T(8,128)S(1)} fusion(f32[4096,256]{1,0:T(8,128)S(1)} %copy-done.2, f32[4096,256]{1,0:T(8,128)S(1)} %bitcast.227), kind=kOutput, calls=%fused_computation.53 | convolution fusion | flops 3221291008 | bytes 8650752 | tf_op jit(solution)/shard_map/dot_general | solution.py:123
  239.3 14.8 %all_to_all.45 = f32[16,1,8192]{2,1,0:T(1,128)S(1)} all-to-all(f32[16,1,8192]{2,1,0:T(1,128)S(1)} %all_to_all.32), channel_id=1, replica_groups=mesh['comp'=8,'blk'=16] {'blk'}, dimensions={0} | all-to-all | bytes 1048576 | tf_op jit(solution)/shard_map/all_to_all | solution.py:62
  255.7 4.0 all-to-all-start.3
  259.6 8.9 %all-to-all-done.3 = f32[16,1,8192]{2,1,0:T(1,128)S(1)} async-done(((f32[16,1,8192]{2,1,0:T(1,128)}), f32[16,1,8192]{2,1,0:T(1,128)S(1)}, u32[]{:S(2)}, u32[]{:S(2)}) %all-to-all-start.3) | async-done | bytes 524320 | tf_op jit(solution)/shard_map/all_to_all | solution.py:40
  270.1 11.7 %cholesky.206 = f32[128,128]{1,0:T(8,128)S(1)} custom-call(f32[128,128]{1,0:T(8,128)S(1)} %cholesky.273), custom_call_target="Cholesky" | custom-call | tf_op jit(solution)/shard_map/jit(cholesky)/cholesky | solution.py:93
  281.9 9.8 %custom-call.17 = f32[1,128,128]{1,2,0:T(8,128)S(1)} custom-call(f32[1,128,128]{2,1,0:T(8,128)S(1)} %get-tuple-element.85), custom_call_target="InvertDiagBlocksLowerTriangular" | custom-call | tf_op jit(solution)/shard_map/jit(cholesky)/cholesky | solution.py:93
  292.2 11.7 %cholesky.223 = f32[128,128]{1,0:T(8,128)S(1)} custom-call(f32[128,128]{1,0:T(8,128)S(1)} %convolution_subtract_fusion.4), custom_call_target="Cholesky" | custom-call | tf_op jit(solution)/shard_map/jit(cholesky)/cholesky | solution.py:93
  306.7 4.2 while.7
  307.4 1.4 bitcast_dynamic-update-slice_fusion.7
  309.5 1.4 bitcast_dynamic-update-slice_fusion.7
  310.9 19.9 %custom-call.18 = f32[2,128,128]{1,2,0:T(8,128)S(1)} custom-call(f32[2,128,128]{2,1,0:T(8,128)S(1)} %get-tuple-element.26), custom_call_target="InvertDiagBlocksLowerTriangular" | custom-call | tf_op jit(solution)/shard_map/triangular_solve/custom-call.0 | solution.py:95
  331.7 5.6 %fusion.51 = f32[4096,256]{1,0:T(8,128)S(1)} fusion(f32[4096,256]{1,0:T(8,128)} %copy-done.1, f32[128,256]{1,0:T(8,128)S(1)} %fusion.63, f32[128,256]{1,0:T(8,128)S(1)} %fusion.54), kind=kOutput, calls=%fused_computation.88 | convolution fusion | flops 3221291008 | bytes 8650752 | tf_op jit(solution)/shard_map/dot_general | solution.py:138
  337.3 7.3 %fusion.9 = f32[32,256,128]{2,1,0:T(8,128)S(1)} fusion(f32[32,128,256]{2,1,0:T(8,128)S(1)} %bitcast.221, f32[1,32,128,128]{3,2,1,0:T(8,128)S(1)} %copy-done.22), kind=kOutput, calls=%fused_computation.28 | convolution fusion | flops 1610612736 | bytes 10485760 | tf_op jit(solution)/shard_map/bkm,bkl->bml/dot_general | solution.py:145
  344.6 5.3 %fusion.31 = f32[256,128,16]{1,2,0:T(8,128)} fusion(f32[32,256,128]{2,1,0:T(8,128)S(1)} %fusion.9, s32[32]{0:T(128)S(1)} %bitcast.232), kind=kOutput, calls=%fused_computation.50 | convolution fusion | flops 201851392 | bytes 6291584 | tf_op jit(solution)/shard_map/bj,bml->mjl/dot_general | solution.py:155
  349.9 4.8 %all-to-all-start.4 = ((f32[16,256,128]{2,1,0:T(8,128)}), f32[16,256,128]{2,1,0:T(8,128)}, u32[]{:S(2)}, u32[]{:S(2)}) async-start(f32[16,256,128]{2,1,0:T(8,128)} %bitcast.228), calls=%async_computation.4 | async-start | bytes 4194304 | tf_op jit(solution)/shard_map/all_to_all | solution.py:62
  355.8 11.7 %cholesky.240 = f32[128,128]{1,0:T(8,128)S(1)} custom-call(f32[128,128]{1,0:T(8,128)S(1)} %cholesky.276), custom_call_target="Cholesky" | custom-call | tf_op jit(solution)/shard_map/jit(cholesky)/cholesky | solution.py:93
  367.6 9.8 %custom-call.19 = f32[1,128,128]{1,2,0:T(8,128)S(1)} custom-call(f32[1,128,128]{2,1,0:T(8,128)S(1)} %get-tuple-element.81), custom_call_target="InvertDiagBlocksLowerTriangular" | custom-call | tf_op jit(solution)/shard_map/jit(cholesky)/cholesky | solution.py:93
  377.9 11.7 %cholesky.257 = f32[128,128]{1,0:T(8,128)S(1)} custom-call(f32[128,128]{1,0:T(8,128)S(1)} %convolution_subtract_fusion.3), custom_call_target="Cholesky" | custom-call | tf_op jit(solution)/shard_map/jit(cholesky)/cholesky | solution.py:93
  389.6 1.7 reduce_sum.38
  391.3 1.5 broadcast_in_dim.22
  392.8 6.9 %all-to-all-start.5 = ((f32[16,256,128]{2,1,0:T(8,128)}), f32[16,256,128]{2,1,0:T(8,128)}, u32[]{:S(2)}, u32[]{:S(2)}) async-start(f32[16,256,128]{2,1,0:T(8,128)} %broadcast_in_dim.22), calls=%async_computation.5 | async-start | bytes 4194304 | tf_op jit(solution)/shard_map/all_to_all | solution.py:40
  402.3 3.8 while.8
  406.1 19.7 %custom-call.20 = f32[2,128,128]{1,2,0:T(8,128)S(1)} custom-call(f32[2,128,128]{2,1,0:T(8,128)S(1)} %get-tuple-element.27), custom_call_target="InvertDiagBlocksLowerTriangular" | custom-call | tf_op jit(solution)/shard_map/triangular_solve/custom-call.0 | solution.py:95
  426.7 4.0 fusion.27
  430.7 3.6 fusion.93
  434.4 1.6 fusion.40
  436.3 38.8 %all_to_all.46 = f32[8,4,128,128]{3,1,2,0:T(4,128)} all-to-all(f32[8,4,128,128]{3,1,2,0:T(4,128)S(1)} %copy.42), channel_id=1, replica_groups=mesh['comp'=8,'blk'=16] {'comp'}, dimensions={0} | all-to-all | bytes 4194304 | tf_op jit(solution)/shard_map/all_to_all | solution.py:62
  475.1 2.0 reduce_sum.39
  (151 shorter events, 33.7 us)
Async XLA Ops:
  0.6 9.1 %copy-start = (f32[1,32,128,128]{3,2,1,0:T(8,128)S(1)}, f32[1,32,128,128]{3,2,1,0:T(8,128)}, u32[]{:S(2)}) copy-start(f32[1,32,128,128]{3,2,1,0:T(8,128)} %param.11) | copy-start | bytes 6291460
  1.8 21.0 %collective-permute-start = (f32[128,256]{1,0:T(8,128)S(1)}, f32[128,256]{1,0:T(8,128)S(1)}, u32[]{:S(2)}, u32[]{:S(2)}) collective-permute-start(f32[128,256]{1,0:T(8,128)S(1)} %get-tuple-element.77), channel_id=1, source_target_pairs={{0,1},{1,2},{2,3},{3,4},{4,5},{5,6},{6,7},{7,8},{8,9},{9,10},{10,1... | collective-permute-start | bytes 393224 | tf_op jit(solution)/shard_map/ppermute | solution.py:25
  6.2 16.6 %collective-permute-start.2 = (f32[128,256]{1,0:T(8,128)S(1)}, f32[128,256]{1,0:T(8,128)S(1)}, u32[]{:S(2)}, u32[]{:S(2)}) collective-permute-start(f32[128,256]{1,0:T(8,128)S(1)} %get-tuple-element.76), channel_id=1, source_target_pairs={{1,0},{2,1},{3,2},{4,3},{5,4},{6,5},{7,6},{8,7},{9,8},{10,9},{11,1... | collective-permute-start | bytes 393224 | tf_op jit(solution)/shard_map/ppermute | solution.py:28
  8.4 23.8 %collective-permute-start.1 = (f32[1,128,128]{1,2,0:T(8,128)S(1)}, f32[1,128,128]{1,2,0:T(8,128)S(1)}, u32[]{:S(2)}, u32[]{:S(2)}) collective-permute-start(f32[1,128,128]{1,2,0:T(8,128)S(1)} %bitcast.231), channel_id=1, source_target_pairs={{1,0},{2,1},{3,2},{4,3},{5,4},{6,5},{7,6},{8,7},{9,8},{10,9},{11,1... | collective-permute-start | bytes 196616 | tf_op jit(solution)/shard_map/ppermute | solution.py:17
  9.7 8.2 %copy-start.9 = (f32[1,32,128,128]{3,2,1,0:T(8,128)S(1)}, f32[1,32,128,128]{3,2,1,0:T(8,128)}, u32[]{:S(2)}) copy-start(f32[1,32,128,128]{3,2,1,0:T(8,128)} %param.12) | copy-start | bytes 6291460
  22.8 4.1 copy-start.10
  26.9 5.3 %copy-start.13 = (f32[1,31,128,128]{2,3,1,0:T(8,128)S(1)}, f32[1,31,128,128]{2,3,1,0:T(8,128)}, u32[]{:S(2)}) copy-start(f32[1,31,128,128]{2,3,1,0:T(8,128)} %copy.48) | copy-start | bytes 6094852
  32.2 6.7 %copy-start.3 = (f32[1,4096,256]{2,1,0:T(8,128)S(1)}, f32[1,4096,256]{2,1,0:T(8,128)}, u32[]{:S(2)}) copy-start(f32[1,4096,256]{2,1,0:T(8,128)} %param.10) | copy-start | bytes 12582916
  39.7 5.4 %copy-start.4 = (f32[4096,256]{1,0:T(8,128)}, f32[4096,256]{1,0:T(8,128)S(1)}, u32[]{:S(2)}) copy-start(f32[4096,256]{1,0:T(8,128)S(1)} %bitcast_subtract_fusion.1) | copy-start | bytes 12582916
  45.1 18.9 %collective-permute-start.3 = (f32[128,256]{1,0:T(8,128)S(1)}, f32[128,256]{1,0:T(8,128)S(1)}, u32[]{:S(2)}, u32[]{:S(2)}) collective-permute-start(f32[128,256]{1,0:T(8,128)S(1)} %get-tuple-element.73), channel_id=1, source_target_pairs={{0,1},{1,2},{2,3},{3,4},{4,5},{5,6},{6,7},{7,8},{8,9},{9,10},{10,1... | collective-permute-start | bytes 393224 | tf_op jit(solution)/shard_map/ppermute | solution.py:25
  49.9 14.1 %collective-permute-start.4 = (f32[128,256]{1,0:T(8,128)S(1)}, f32[128,256]{1,0:T(8,128)S(1)}, u32[]{:S(2)}, u32[]{:S(2)}) collective-permute-start(f32[128,256]{1,0:T(8,128)S(1)} %get-tuple-element.72), channel_id=1, source_target_pairs={{1,0},{2,1},{3,2},{4,3},{5,4},{6,5},{7,6},{8,7},{9,8},{10,9},{11,1... | collective-permute-start | bytes 393224 | tf_op jit(solution)/shard_map/ppermute | solution.py:28
  51.4 1.6 copy-start.19
  53.0 4.2 copy-start.5
  64.0 4.5 copy-start.11
  68.5 5.3 %copy-start.14 = (f32[1,31,128,128]{2,3,1,0:T(8,128)S(1)}, f32[1,31,128,128]{2,3,1,0:T(8,128)}, u32[]{:S(2)}) copy-start(f32[1,31,128,128]{2,3,1,0:T(8,128)} %copy.48) | copy-start | bytes 6094852
  68.5 5.3 %copy-start.17 = (f32[32,256,128]{1,2,0:T(8,128)S(1)}, f32[32,256,128]{1,2,0:T(8,128)}, u32[]{:S(2)}) copy-start(f32[32,256,128]{1,2,0:T(8,128)} %fusion.23) | copy-start | bytes 12582916
  73.8 8.2 %copy-start.6 = (f32[1,4096,256]{2,1,0:T(8,128)S(1)}, f32[1,4096,256]{2,1,0:T(8,128)}, u32[]{:S(2)}) copy-start(f32[1,4096,256]{2,1,0:T(8,128)} %copy-done.5) | copy-start | bytes 12582916
  80.1 1.9 copy-start.7
  90.6 19.6 %all-to-all-start = ((f32[16,1,8192]{2,1,0:T(1,128)}), f32[16,1,8192]{2,1,0:T(1,128)S(1)}, u32[]{:S(2)}, u32[]{:S(2)}) async-start(f32[16,1,8192]{2,1,0:T(1,128)} %all_to_all.29), calls=%async_computation | async-start | bytes 1048576 | tf_op jit(solution)/shard_map/all_to_all | solution.py:62
  111.7 12.5 %all-to-all-start.1 = ((f32[16,1,8192]{2,1,0:T(1,128)}), f32[16,1,8192]{2,1,0:T(1,128)S(1)}, u32[]{:S(2)}, u32[]{:S(2)}) async-start(f32[16,1,8192]{2,1,0:T(1,128)} %broadcast_in_dim.18), calls=%async_computation.1 | async-start | bytes 1048576 | tf_op jit(solution)/shard_map/all_to_all | solution.py:40
  185.5 5.6 %copy-start.8 = (f32[32,128,256]{2,1,0:T(8,128)S(1)}, f32[32,128,256]{2,1,0:T(8,128)}, u32[]{:S(2)}) copy-start(f32[32,128,256]{2,1,0:T(8,128)} %copy-done.7) | copy-start | bytes 12582916
  191.2 3.7 copy-start.20
  194.8 13.9 %copy-start.1 = (f32[4096,256]{1,0:T(8,128)}, f32[4096,256]{1,0:T(8,128)S(1)}, u32[]{:S(2)}) copy-start(f32[4096,256]{1,0:T(8,128)S(1)} %fusion) | copy-start | bytes 12582916
  204.7 11.1 %collective-permute-start.5 = (f32[128,256]{1,0:T(8,128)S(1)}, f32[128,256]{1,0:T(8,128)S(1)}, u32[]{:S(2)}, u32[]{:S(2)}) collective-permute-start(f32[128,256]{1,0:T(8,128)S(1)} %get-tuple-element.69), channel_id=1, source_target_pairs={{0,1},{1,2},{2,3},{3,4},{4,5},{5,6},{6,7},{7,8},{8,9},{9,10},{10,1... | collective-permute-start | bytes 393224 | tf_op jit(solution)/shard_map/ppermute | solution.py:25
  206.9 8.9 %collective-permute-start.6 = (f32[128,256]{1,0:T(8,128)S(1)}, f32[128,256]{1,0:T(8,128)S(1)}, u32[]{:S(2)}, u32[]{:S(2)}) collective-permute-start(f32[128,256]{1,0:T(8,128)S(1)} %get-tuple-element.68), channel_id=1, source_target_pairs={{1,0},{2,1},{3,2},{4,3},{5,4},{6,5},{7,6},{8,7},{9,8},{10,9},{11,1... | collective-permute-start | bytes 393224 | tf_op jit(solution)/shard_map/ppermute | solution.py:28
  215.8 4.1 copy-start.12
  219.9 5.5 %copy-start.15 = (f32[1,31,128,128]{2,3,1,0:T(8,128)S(1)}, f32[1,31,128,128]{2,3,1,0:T(8,128)}, u32[]{:S(2)}) copy-start(f32[1,31,128,128]{2,3,1,0:T(8,128)} %copy.48) | copy-start | bytes 6094852
  219.9 5.5 %copy-start.18 = (f32[32,256,128]{1,2,0:T(8,128)S(1)}, f32[32,256,128]{1,2,0:T(8,128)}, u32[]{:S(2)}) copy-start(f32[32,256,128]{1,2,0:T(8,128)} %fusion.21) | copy-start | bytes 12582916
  225.4 6.2 %copy-start.2 = (f32[4096,256]{1,0:T(8,128)S(1)}, f32[4096,256]{1,0:T(8,128)}, u32[]{:S(2)}) copy-start(f32[4096,256]{1,0:T(8,128)} %copy-done.1) | copy-start | bytes 12582916
  255.7 12.9 %all-to-all-start.3 = ((f32[16,1,8192]{2,1,0:T(1,128)}), f32[16,1,8192]{2,1,0:T(1,128)S(1)}, u32[]{:S(2)}, u32[]{:S(2)}) async-start(f32[16,1,8192]{2,1,0:T(1,128)} %broadcast_in_dim.19), calls=%async_computation.3 | async-start | bytes 1048576 | tf_op jit(solution)/shard_map/all_to_all | solution.py:40
  331.6 5.6 %copy-start.22 = (f32[1,32,128,128]{3,2,1,0:T(8,128)S(1)}, f32[1,32,128,128]{3,2,1,0:T(8,128)}, u32[]{:S(2)}) copy-start(f32[1,32,128,128]{3,2,1,0:T(8,128)} %param.14) | copy-start | bytes 6291460
  337.3 7.3 %copy-start.16 = (f32[4096,256]{1,0:T(8,128)}, f32[4096,256]{1,0:T(8,128)S(1)}, u32[]{:S(2)}) copy-start(f32[4096,256]{1,0:T(8,128)S(1)} %fusion.51) | copy-start | bytes 12582916
  337.3 7.3 %copy-start.23 = (s32[1,32]{1,0:T(1,128)S(1)}, s32[1,32]{1,0:T(1,128)}, u32[]{:S(2)}) copy-start(s32[1,32]{1,0:T(1,128)} %param.15) | copy-start | bytes 388
  349.9 39.7 %all-to-all-start.4 = ((f32[16,256,128]{2,1,0:T(8,128)}), f32[16,256,128]{2,1,0:T(8,128)}, u32[]{:S(2)}, u32[]{:S(2)}) async-start(f32[16,256,128]{2,1,0:T(8,128)} %bitcast.228), calls=%async_computation.4 | async-start | bytes 4194304 | tf_op jit(solution)/shard_map/all_to_all | solution.py:62
  355.6 37.2 %copy-start.21 = (f32[256,256]{1,0:T(8,128)}, f32[256,256]{1,0:T(8,128)S(1)}, u32[]{:S(2)}) copy-start(f32[256,256]{1,0:T(8,128)S(1)} %fusion.49) | copy-start | bytes 786436
  392.8 33.9 %all-to-all-start.5 = ((f32[16,256,128]{2,1,0:T(8,128)}), f32[16,256,128]{2,1,0:T(8,128)}, u32[]{:S(2)}, u32[]{:S(2)}) async-start(f32[16,256,128]{2,1,0:T(8,128)} %broadcast_in_dim.22), calls=%async_computation.5 | async-start | bytes 4194304 | tf_op jit(solution)/shard_map/all_to_all | solution.py:40
  426.7 7.7 %copy-start.24 = (s32[1,16]{1,0:T(1,128)S(1)}, s32[1,16]{1,0:T(1,128)}, u32[]{:S(2)}) copy-start(s32[1,16]{1,0:T(1,128)} %param.16) | copy-start | bytes 196
where the time goes:
time: 483 us; the launch traced here: 478 us
  other arithmetic  181 us (37%)
  matrix products  132 us (27%)
  blocking collectives  53.6 us (11%)
  starting transfers between devices  46.8 us (10%)
  local copies, waits for them, and re-layouts  31.5 us (7%)
  waiting for transfers between devices  27 us (6%)
  between operations  5.56 us (1%)
    another operation x20, other arithmetic, lower_inverse(): factor = jnp.linalg.cholesky(matrix)  103 us
    another operation x7, other arithmetic, lower_inverse(): lax.linalg.triangular_solve(factor, unit_matrix, left_side=True, lower=True)  59.5 us
    all_to_all x2, blocking collectives, sent_and_summed(): pieces = lax.all_to_all(split_up(array, dim, peers), axis, 0, 0, tiled=True)  53.6 us
    dot_general x8, matrix products, block_product(): return jnp.einsum('bij,bjm->bim', blocks, vectors, precision=highest)  43.7 us
    dot_general x4, matrix products, gram_matrix(): return jnp.dot(left.T, right, precision=highest) / dof_count  27.9 us
    dot_general x3, matrix products, stiff_apply(): jnp.einsum('bji,bjm->bim', link_after, extended[2:], precision=highest)  19 us
    all_to_all x3, waiting for transfers between devices, copy_for_each(): return lax.all_to_all(copies, axis, split_axis=0, concat_axis=0, tiled=True)  17.8 us
    all_to_all x2, starting transfers between devices, sent_and_summed(): pieces = lax.all_to_all(split_up(array, dim, peers), axis, 0, 0, tiled=True)  15.3 us
  transfers between devices with their start and end apart: 12, of which 3 were waited for; matrix products, arithmetic and copies ran while one was open for 21% of the time, Pallas kernels for 0%

commit v1 on v0

v1 whole, which is shorter than its diff:
```python
import functools

import jax
import jax.numpy as jnp
from jax import lax
from jax.experimental import pallas as pl
from jax.experimental.pallas import tpu as pltpu
from jax.sharding import PartitionSpec as P

BF = jnp.bfloat16
F32 = jnp.float32
STEP = 0.15
MESH = pl.DeviceIdType.MESH
HI = lax.Precision.HIGHEST
MIB = 1 << 20


def split(x):
    hi = x.astype(BF)
    lo = (x - hi.astype(F32)).astype(BF)
    return hi, lo


def mm(a, b):
    return jnp.dot(a, b, preferred_element_type=F32)


def mmh(a, b):
    return jnp.dot(a, b, preferred_element_type=F32, precision=HI)


def chain_kernel(nb, count, x_ref, d_ref, e_ref, yh_ref, yl_ref, zh_ref, zl_ref,
                 xh, xl, fh, fl, eyh, eyl, ah, al, edge, halo, enext, send_sem, recv_sem):
    pairs = nb // 2
    rows = nb * 128
    me = lax.axis_index("blk")
    left, right = lax.rem(me + count - 1, count), lax.rem(me + 1, count)
    barrier = pltpu.get_barrier_semaphore()
    for peer in (left, right):
        pl.semaphore_signal(barrier, inc=1, device_id={"blk": peer}, device_id_type=MESH)
    pl.semaphore_wait(barrier, 2)

    def send(src, dst, slot, peer):
        copy = pltpu.make_async_remote_copy(
            src_ref=src, dst_ref=dst, send_sem=send_sem.at[slot], recv_sem=recv_sem.at[slot],
            device_id={"blk": peer}, device_id_type=MESH)
        copy.start()
        return copy

    copies = [
        send(e_ref.at[0], enext, 6, left),
        send(x_ref.at[pl.ds(rows - 128, 128)], halo.at[0], 0, right),
        send(x_ref.at[pl.ds(0, 128)], halo.at[1], 1, left),
    ]
    has_left = me > 0
    has_right = me < count - 1

    def put_a(p, row, col, block):
        hi, lo = split(block)
        ah[p, row * 128:(row + 1) * 128, col * 128:(col + 1) * 128] = hi
        al[p, row * 128:(row + 1) * 128, col * 128:(col + 1) * 128] = lo

    zero = jnp.zeros((128, 128), F32)

    def build(p, _):
        b = 2 * p
        e0 = e_ref[b]
        e0 = jnp.where(jnp.logical_or(has_left, p > 0), e0, 0.0)
        e1 = e_ref[b + 1]
        put_a(p, 0, 0, e0)
        put_a(p, 0, 1, d_ref[b])
        put_a(p, 0, 2, e1.T)
        put_a(p, 0, 3, zero)
        put_a(p, 1, 0, zero)
        put_a(p, 1, 1, e1)
        put_a(p, 1, 2, d_ref[b + 1])
        e2 = e_ref[jnp.minimum(b + 2, nb - 1)]
        put_a(p, 1, 3, e2.T)
        r = pl.multiple_of(p * 256, 256)
        hi, lo = split(x_ref[pl.ds(r, 256), :])
        o = pl.multiple_of(r + 128, 128)
        xh[pl.ds(o, 256), :] = hi
        xl[pl.ds(o, 256), :] = lo
        return 0

    lax.fori_loop(0, pairs, build, 0)

    def product(vh, vl, p):
        r = pl.multiple_of(p * 256, 256)
        h = vh[pl.ds(r, 512), :]
        l = vl[pl.ds(r, 512), :]
        a = ah[p]
        return mm(a, h) + mm(a, l) + mm(al[p], h)

    def own(p):
        return pl.ds(pl.multiple_of(p * 256 + 128, 128), 256)

    def apply_f(p):
        acc = product(xh, xl, p)
        x = x_ref[pl.ds(pl.multiple_of(p * 256, 256), 256), :]
        f = x * (1.0 / 256) - acc * (STEP / 256)
        hi, lo = split(f)
        fh[own(p), :] = hi
        fl[own(p), :] = lo
        return f

    def apply_y(p):
        acc = product(fh, fl, p)
        f = fh[own(p), :].astype(F32) + fl[own(p), :].astype(F32)
        y = f - acc * STEP
        hi, lo = split(y)
        eyh[own(p), :] = hi
        eyl[own(p), :] = lo
        o = pl.ds(pl.multiple_of(p * 256, 256), 256)
        yh_ref[o, :] = hi
        yl_ref[o, :] = lo
        return y

    def apply_z(p):
        acc = product(eyh, eyl, p)
        hi, lo = split(acc)
        o = pl.ds(pl.multiple_of(p * 256, 256), 256)
        zh_ref[o, :] = hi
        zl_ref[o, :] = lo
        return acc

    for rnd, (fn, vh, vl) in enumerate(((apply_f, xh, xl), (apply_y, fh, fl), (apply_z, eyh, eyl))):
        def body(p, _, fn=fn):
            fn(p)
            return 0

        lax.fori_loop(1, pairs - 1, body, 0)
        if rnd == 0:
            copies[0].wait()
            e2 = jnp.where(has_right, enext[...], 0.0)
            put_a(pairs - 1, 1, 3, e2.T)
        copies[2 * rnd + 1].wait()
        hi, lo = split(jnp.where(has_left, halo[2 * rnd], 0.0))
        vh[0:128, :] = hi
        vl[0:128, :] = lo
        copies[2 * rnd + 2].wait()
        hi, lo = split(jnp.where(has_right, halo[2 * rnd + 1], 0.0))
        vh[rows + 128:rows + 256, :] = hi
        vl[rows + 128:rows + 256, :] = lo
        last = fn(pairs - 1)
        if rnd < 2:
            edge[2 * rnd] = last[128:, :]
            copies.append(send(edge.at[2 * rnd], halo.at[2 * rnd + 2], 2 * rnd + 2, right))
        first = fn(0)
        if rnd < 2:
            edge[2 * rnd + 1] = first[:128, :]
            copies.append(send(edge.at[2 * rnd + 1], halo.at[2 * rnd + 3], 2 * rnd + 3, left))


def chain(x, d, e, count):
    nb = d.shape[0]
    rows = nb * 128
    ext = pltpu.VMEM((rows + 256, 256), BF)
    vm = pl.BlockSpec(memory_space=pltpu.VMEM)
    out = jax.ShapeDtypeStruct((rows, 256), BF)
    return pl.pallas_call(
        functools.partial(chain_kernel, nb, count),
        out_shape=(out,) * 4,
        in_specs=[vm] * 3,
        out_specs=(vm,) * 4,
        scratch_shapes=[ext] * 6 + [
            pltpu.VMEM((nb // 2, 256, 512), BF),
            pltpu.VMEM((nb // 2, 256, 512), BF),
            pltpu.VMEM((4, 128, 256), F32),
            pltpu.VMEM((6, 128, 256), F32),
            pltpu.VMEM((128, 128), F32),
            pltpu.SemaphoreType.DMA((7,)),
            pltpu.SemaphoreType.DMA((7,)),
        ],
        compiler_params=pltpu.CompilerParams(
            collective_id=0, has_side_effects=True, vmem_limit_bytes=60 * MIB),
        name="chain",
    )(x, d, e)


def gram_kernel(ids, yh_ref, yl_ref, zh_ref, zl_ref, m_ref, c_ref, ps_ref, w_ref):
    p = pl.program_id(0)

    @pl.when(p == 0)
    def _():
        ps_ref[...] = jnp.zeros_like(ps_ref)
        w_ref[...] = jnp.zeros_like(w_ref)

    yh, yl = yh_ref[...], yl_ref[...]
    parts = []
    for q in range(2):
        mh, ml = split(m_ref[q])
        left = jnp.concatenate(
            [jnp.concatenate([mh, mh], 1), jnp.concatenate([ml, ml], 1)], 0)
        s = slice(q * 128, (q + 1) * 128)
        both = mm(left, jnp.concatenate([yh[s], yl[s]], 0))
        parts.append(both[:128] + both[128:])
    myh, myl = split(jnp.concatenate(parts, 0))
    yth, ytl = yh.T, yl.T
    hi = jnp.concatenate([myh, zh_ref[...]], 1)
    lo = jnp.concatenate([myl, zl_ref[...]], 1)
    ps_ref[...] += mm(yth, hi) + mm(yth, lo) + mm(ytl, hi)
    for q in range(2):
        ch, cl = split(c_ref[q])
        cc = jnp.concatenate([ch, cl], 1)
        s = slice(q * 128, (q + 1) * 128)
        both = mm(jnp.concatenate([yth[:, s], ytl[:, s]], 1), jnp.concatenate([cc, cc], 0))
        j = ids[2 * p + q]
        term = jnp.where(j < 16, both[:, :128] + both[:, 128:], 0.0)
        slot = jnp.minimum(j, 15)
        w_ref[slot] = w_ref[slot] + term


def gram(ids, yh, yl, zh, zl, m, c):
    nb = m.shape[0]
    tile = pl.BlockSpec((256, 256), lambda p, ids: (p, 0))
    blocks = pl.BlockSpec((2, 128, 128), lambda p, ids: (p, 0, 0))
    return pl.pallas_call(
        gram_kernel,
        out_shape=(jax.ShapeDtypeStruct((256, 512), F32), jax.ShapeDtypeStruct((16, 256, 128), F32)),
        grid_spec=pltpu.PrefetchScalarGridSpec(
            num_scalar_prefetch=1,
            grid=(nb // 2,),
            in_specs=[tile] * 4 + [blocks] * 2,
            out_specs=(pl.BlockSpec((256, 512), lambda p, ids: (0, 0)),
                       pl.BlockSpec((16, 256, 128), lambda p, ids: (0, 0, 0))),
        ),
        compiler_params=pltpu.CompilerParams(vmem_limit_bytes=40 * MIB),
        name="gram",
    )(ids, yh, yl, zh, zl, m, c)


def diag_inverse(mats):
    size = 64
    groups = size // 8
    sub = lax.broadcasted_iota(jnp.int32, (8, 128), 0)
    lane = lax.broadcasted_iota(jnp.int32, (8, 128), 1)
    state = []
    for mat in mats:
        full = jnp.concatenate([mat, jnp.zeros_like(mat)], 1)
        state.append([
            jnp.where(lane == sub + (64 + 8 * g), 1.0, full[8 * g:8 * g + 8]) for g in range(groups)
        ])
    for k in range(groups):
        cols = [[[jnp.broadcast_to(rows[g][:, 8 * k + c:8 * k + c + 1], (8, 128)) for c in range(8)]
                 for g in range(k, groups)] for rows in state]
        for c in range(8):
            for rows, col in zip(state, cols):
                mine = col[0]
                rs = lax.rsqrt(jnp.broadcast_to(mine[c][c:c + 1, :], (8, 128)))
                u = jnp.broadcast_to(rows[k][c:c + 1, :], (8, 128)) * rs
                heads = {n: jnp.broadcast_to(mine[n][c:c + 1, :], (8, 128)) * rs for n in range(c + 1, 8)}
                for g in range(k, groups):
                    mult = col[g - k][c] * rs
                    if g == k:
                        mult = jnp.where(sub > c, mult, 0.0)
                        rows[g] = jnp.where(sub == c, u, rows[g] - mult * u)
                    else:
                        rows[g] = rows[g] - mult * u
                    for n in range(c + 1, 8):
                        col[g - k][n] = col[g - k][n] - mult * heads[n]
    return [jnp.concatenate(rows, 0) for rows in state]


def factor_kernel(ps_ref, cth_ref, ctl_ref, red_ref, qi_ref, a_ref, x_ref):
    size = 256
    row = lax.broadcasted_iota(jnp.int32, (size, size), 0)
    column = lax.broadcasted_iota(jnp.int32, (size, size), 1)
    for t in range(2):
        g = ps_ref[:, t * size:(t + 1) * size]
        a_ref[t] = (g + g.T) * 0.5
        x_ref[t] = jnp.where(row == column, 1.0, 0.0)
    for k in range(4):
        lo, hi = 64 * k, 64 * (k + 1)
        inv = diag_inverse([a_ref[t, lo:hi, lo:hi] for t in range(2)])
        for t in range(2):
            tri = inv[t][:, 64:]
            xu = mmh(tri, x_ref[t, lo:hi, :])
            x_ref[t, lo:hi, :] = xu
            if k < 3:
                au = mmh(tri, a_ref[t, lo:hi, :])
                low = au[:, hi:].T
                a_ref[t, hi:, :] = a_ref[t, hi:, :] - mmh(low, au)
                x_ref[t, hi:, :] = x_ref[t, hi:, :] - mmh(low, xu)
    ci = x_ref[0]
    ct = ci.T
    red_ref[...] = mmh(mmh(ci, ps_ref[:, size:]), ct)
    qi_ref[...] = x_ref[1]
    h, l = split(ct * 256.0)
    cth_ref[...] = h
    ctl_ref[...] = l


def factor(ps):
    sq = jax.ShapeDtypeStruct((256, 256), F32)
    sb = jax.ShapeDtypeStruct((256, 256), BF)
    vm = pl.BlockSpec(memory_space=pltpu.VMEM)
    return pl.pallas_call(
        factor_kernel,
        out_shape=(sb, sb, sq, sq),
        in_specs=[vm],
        out_specs=(vm,) * 4,
        scratch_shapes=[pltpu.VMEM((2, 256, 256), F32)] * 2,
        compiler_params=pltpu.CompilerParams(vmem_limit_bytes=32 * MIB),
        cost_estimate=pl.CostEstimate(flops=4 * 10**9, bytes_accessed=10**6, transcendentals=0),
        name="factor",
    )(ps)


def modes_kernel(yh_ref, yl_ref, cth_ref, ctl_ref, out_ref):
    h = yh_ref[...]
    out_ref[...] = mm(h, cth_ref[...]) + mm(h, ctl_ref[...]) + mm(yl_ref[...], cth_ref[...])


def modes_of(yh, yl, cth, ctl):
    rows = yh.shape[0]
    t = 512
    tile = pl.BlockSpec((t, 256), lambda p: (p, 0))
    whole = pl.BlockSpec((256, 256), lambda p: (0, 0))
    return pl.pallas_call(
        modes_kernel,
        out_shape=jax.ShapeDtypeStruct((rows, 256), F32),
        grid=(rows // t,),
        in_specs=[tile, tile, whole, whole],
        out_specs=tile,
        name="modes",
    )(yh, yl, cth, ctl)


def condense_kernel(qi_ref, w_ref, out_ref):
    scaled = mmh(qi_ref[...], w_ref[...])
    out_ref[...] = mmh(scaled.T, scaled)


def condense(qi, w):
    vm = pl.BlockSpec(memory_space=pltpu.VMEM)
    return pl.pallas_call(
        condense_kernel,
        out_shape=jax.ShapeDtypeStruct((128, 128), F32),
        in_specs=[vm] * 2,
        out_specs=vm,
        name="condense",
    )(qi, w)


def local(start_modes, stiff_diag, stiff_off, mass_blocks, coupling, interface_block, global_iface):
    count = lax.axis_size("blk")
    yh, yl, zh, zl = chain(start_modes[0], stiff_diag[0], stiff_off[0], count)
    ps, w = gram(interface_block[0], yh, yl, zh, zl, mass_blocks[0], coupling[0])
    ps = lax.psum(ps, "blk")
    mine = lax.psum_scatter(w, "blk", scatter_dimension=0, tiled=False)
    cth, ctl, reduced, qi = factor(ps)
    modes = modes_of(yh, yl, cth, ctl)
    cond = condense(qi, mine)
    pieces = lax.all_to_all(cond.reshape(count, 128 // count, 128), "blk", 0, 0, tiled=True)
    owners = lax.axis_size("comp")
    hot = (jnp.arange(4 * owners, dtype=jnp.int32)[:, None] == global_iface[0][None, :]).astype(F32)
    dense = jnp.einsum("gj,jkl->gkl", hot, pieces, precision=HI)
    slab = jnp.sum(lax.all_to_all(dense.reshape(owners, 4, 128 // count, 128), "comp", 0, 0, tiled=True), 0)
    assembled = lax.all_gather(slab, "blk", axis=1, tiled=True)
    return modes[None], reduced[None], assembled


def solution(mesh):
    in_specs = (
        P("comp", "blk", None),
        P("comp", "blk", None, None),
        P("comp", "blk", None, None),
        P("comp", "blk", None, None),
        P("comp", "blk", None, None),
        P("comp", "blk"),
        P("comp", None),
    )
    out_specs = (P("comp", "blk", None), P("comp", None, None), P("comp", None, None))
    return jax.shard_map(local, mesh=mesh, in_specs=in_specs, out_specs=out_specs, check_vma=False)
```

time: 483 us -> 286 us (0.59)
  other arithmetic: 181 us -> 0.03 us
  matrix products: 132 us -> 0.32 us
  waiting for transfers between devices: 27 us -> 143 us
  Pallas kernels: 0 us -> 74.8 us
  starting transfers between devices: 46.8 us -> 8.46 us
  blocking collectives: 53.6 us -> 27.6 us
  local copies, waits for them, and re-layouts: 31.5 us -> 12.2 us
  between operations: 5.56 us -> 14.1 us
    another operation x27 -> x0, other arithmetic: 163 us -> none  [the longest x20 103 us: lower_inverse(): factor = jnp.linalg.cholesky(matrix)]
    dot_general x25 -> x1, matrix products: 128 us -> 0.32 us  [local(): dense = jnp.einsum('gj,jkl->gkl', hot, pieces, precision=HI)]
    psum x0 -> x1, waiting for transfers between devices: none -> 82.7 us  [local(): ps = lax.psum(ps, 'blk')]
    pallas_call x0 -> x5, Pallas kernels: none -> 74.8 us  [the longest x1 34.9 us: chain(): pl.pallas_call(functools.partial(chain_kernel, nb, count), out_shape=(out...]
    unnamed x0 -> x3, waiting for transfers between devices: none -> 60.2 us
    all_to_all x2 -> x1, blocking collectives: 53.6 us -> 10.9 us  [local(): lax.all_to_all(cond.reshape(count, 128 // count, 128), 'blk', 0, 0, tiled...]
    all_to_all x5 -> x1, waiting for transfers between devices: 27 us -> 0.01 us  [local(): lax.all_to_all(dense.reshape(owners, 4, 128 // count, 128), 'comp', 0, 0,...]
    all_to_all x5 -> x1, starting transfers between devices: 29.7 us -> 8.2 us  [local(): lax.all_to_all(dense.reshape(owners, 4, 128 // count, 128), 'comp', 0, 0,...]
  transfers between devices with their start and end apart: 12 -> 3, of which waited for: 3 -> 2; matrix products, arithmetic and copies ran while one was open for 21% -> 0% of each run, Pallas kernels for 0% -> 8%
where the time goes in v1:
time: 286 us; the launch traced here: 280 us
  waiting for transfers between devices  143 us (50%)
  Pallas kernels  74.8 us (26%)
  blocking collectives  27.6 us (10%)
  between operations  14.1 us (5%)
  local copies, waits for them, and re-layouts  12.2 us (4%)
  starting transfers between devices  8.46 us (3%)
    psum x1, waiting for transfers between devices, local(): ps = lax.psum(ps, 'blk')  82.7 us
    unnamed x3, waiting for transfers between devices  60.2 us
    pallas_call x1, Pallas kernels, chain(): pl.pallas_call(functools.partial(chain_kernel, nb, count), out_shape=(out...  34.9 us
    all_gather x1, blocking collectives, local(): assembled = lax.all_gather(slab, 'blk', axis=1, tiled=True)  16.7 us
    pallas_call x1, Pallas kernels, factor(): pl.pallas_call(factor_kernel, out_shape=(sb, sb, sq, sq), in_specs=[vm],...  14.9 us
    pallas_call x1, Pallas kernels, gram(): pl.pallas_call(gram_kernel, out_shape=(jax.ShapeDtypeStruct((256, 512), F...  14.8 us
    unnamed x25, local copies, waits for them, and re-layouts  11.5 us
    all_to_all x1, blocking collectives, local(): lax.all_to_all(cond.reshape(count, 128 // count, 128), 'blk', 0, 0, tiled...  10.9 us
  transfers between devices with their start and end apart: 3, of which 2 were waited for; matrix products, arithmetic and copies ran while one was open for 0% of the time, Pallas kernels for 8%

profile of v1, /device:TPU:1, one launch (start us, length us, event | category | flops | bytes accessed | tf_op | source)
XLA Modules:
  0.0 280.4 jit_solution(11222137484081227020)
XLA Ops:
  7.2 0.0 all-reduce.3.cloned.1.call-start
  7.2 0.0 copy-start.2
  7.2 0.0 copy-start.9
  7.2 34.9 %chain.1 = (bf16[4096,256]{1,0:T(8,128)(2,1)}, bf16[4096,256]{1,0:T(8,128)(2,1)}, bf16[4096,256]{1,0:T(8,128)(2,1)}, bf16[4096,256]{1,0:T(8,128)(2,1)}) custom-call(f32[4096,256]{1,0:T(8,128)} %bitcast.18, f32[32,128,128]{2,1,0:T(8,128)} %bitcast.21, f32[32,128,128]{2,1,0:T(8,128)} %bitcast.22), custom_call_target="tpu_custom_call" | custom-call | tf_op jit(solution)/shard_map/chain/pallas_call | solution.py:161
  42.2 0.0 copy-done.2
  42.2 0.0 copy-done.9
  42.2 0.0 copy-start
  42.2 1.6 copy-done
  43.8 0.0 copy-start.1
  43.8 1.6 copy-done.1
  45.4 0.0 copy-start.3
  45.4 1.6 copy-done.3
  47.0 0.0 copy-start.4
  47.0 1.6 copy-done.4
  48.5 14.8 %gram.1 = (f32[256,512]{1,0:T(8,128)}, f32[16,256,128]{2,1,0:T(8,128)S(1)}) custom-call(s32[32]{0:T(128)S(1)} %bitcast.17, bf16[4096,256]{1,0:T(8,128)(2,1)S(1)} %copy-done, bf16[4096,256]{1,0:T(8,128)(2,1)S(1)} %copy-done.1, bf16[4096,256]{1,0:T(8,128)(2,1)S(1)} %copy-done.3, bf16[4096,256]{1,0:T(8,128)(2,1)S(1)} %copy-done.4, ...), custom_call_target="tpu_custom_call" | custom-call | tf_op jit(solution)/shard_map/gram/pallas_call | solution.py:218
  63.3 0.0 copy-start.5
  63.3 1.3 copy-done.5
  64.7 0.0 all-reduce.3.cloned.1.call-update
  64.7 0.2 reduce-scatter.4.cloned.1.call-start
  64.9 0.5 reduce-scatter.4.cloned.1.call-update
  65.4 82.7 %all-reduce.3.cloned.1.call-done.ps_ref = f32[256,512]{1,0:T(8,128)} async-done(((f32[256,512]{1,0:T(8,128)}), f32[256,512]{1,0:T(8,128)}) %all-reduce.3.cloned.1.call-update) | async-done | bytes 524304 | tf_op jit(solution)/shard_map/psum | solution.py:350
  148.1 0.0 copy-start.10
  148.1 1.0 copy-done.10
  149.2 0.0 copy-start.11
  149.2 14.9 %factor.1 = (bf16[256,256]{1,0:T(8,128)(2,1)S(1)}, bf16[256,256]{1,0:T(8,128)(2,1)S(1)}, f32[256,256]{1,0:T(8,128)}, f32[256,256]{1,0:T(8,128)S(1)}) custom-call(f32[256,512]{1,0:T(8,128)S(1)} %copy-done.10), custom_call_target="tpu_custom_call" | custom-call | flops 4000000000 | bytes 1000000 | tf_op jit(solution)/shard_map/factor/pallas_call | solution.py:298
  164.1 0.0 copy-start.6
  164.1 0.7 copy-done.6
  164.8 0.0 copy-start.7
  164.8 0.7 copy-done.7
  165.4 0.0 copy-start.8
  165.4 0.7 copy-done.8
  166.1 59.7 %reduce-scatter.4.cloned.1.call-done = f32[1,256,128]{2,1,0:T(8,128)} async-done(((f32[16,256,128]{2,1,0:T(8,128)}), f32[1,256,128]{2,1,0:T(8,128)}) %reduce-scatter.4.cloned.1.call-update) | async-done | bytes 131088
  225.8 2.4 condense.1
  228.2 10.9 %all_to_all.10 = f32[16,8,128]{2,1,0:T(8,128)S(1)} all-to-all(f32[16,8,128]{2,1,0:T(8,128)} %bitcast.24), channel_id=1, replica_groups=mesh['comp'=8,'blk'=16] {'blk'}, dimensions={0} | all-to-all | bytes 131072 | tf_op jit(solution)/shard_map/all_to_all | solution.py:355
  239.1 0.0 copy-done.11
  239.1 0.3 fusion
  239.4 0.7 copy.16
  240.1 8.2 %all-to-all-start.1 = ((f32[8,4,8,128]{3,1,2,0:T(4,128)}), f32[8,4,8,128]{3,1,2,0:T(4,128)S(1)}, u32[]{:S(2)}, u32[]{:S(2)}) async-start(f32[8,4,8,128]{3,1,2,0:T(4,128)} %copy.16), calls=%async_computation.1 | async-start | bytes 262144 | tf_op jit(solution)/shard_map/all_to_all | solution.py:359
  248.3 7.8 %modes.1 = f32[4096,256]{1,0:T(8,128)} custom-call(bf16[4096,256]{1,0:T(8,128)(2,1)} %get-tuple-element.13.yh_ref, bf16[4096,256]{1,0:T(8,128)(2,1)} %get-tuple-element.14.yl_ref, bf16[256,256]{1,0:T(8,128)(2,1)} %copy-done.7, bf16[256,256]{1,0:T(8,128)(2,1)} %copy-done.8), custom_call_target="tpu_custom_call" | custom-call | tf_op jit(solution)/shard_map/modes/pallas_call | solution.py:320
  256.1 0.0 all-to-all-done.1
  256.1 16.7 %all_gather.3 = f32[4,128,128]{2,0,1:T(4,128)S(1)} all-gather(f32[4,8,128]{2,0,1:T(4,128)S(1)} %reduce_sum.9), channel_id=1, replica_groups=mesh['comp'=8,'blk'=16] {'blk'}, dimensions={1}, use_global_device_ids=true | all-gather | bytes 278528 | tf_op jit(solution)/shard_map/all_gather | solution.py:360
  272.9 0.7 copy.18
  (1 shorter events, 0.0 us)
Async XLA Ops:
  7.2 141.0 %all-reduce.3.cloned.1.call-start = ((), (), s32[]{:S(2)}) async-start(), calls=%async_computation.3 | async-start | bytes 1048576 | tf_op jit(solution)/shard_map/psum | solution.py:350
  7.2 34.9 %copy-start.2 = (f32[1,32,128,128]{3,2,1,0:T(8,128)S(1)}, f32[1,32,128,128]{3,2,1,0:T(8,128)}, u32[]{:S(2)}) copy-start(f32[1,32,128,128]{3,2,1,0:T(8,128)} %param.10) | copy-start | bytes 6291460
  7.2 34.9 %copy-start.9 = (s32[1,32]{1,0:T(1,128)S(1)}, s32[1,32]{1,0:T(1,128)}, u32[]{:S(2)}) copy-start(s32[1,32]{1,0:T(1,128)} %param.12) | copy-start | bytes 388
  42.2 1.6 copy-start
  43.8 1.6 copy-start.1
  45.4 1.6 copy-start.3
  47.0 1.6 copy-start.4
  63.3 1.3 copy-start.5
  64.7 161.1 %reduce-scatter.4.cloned.1.call-start = ((), (), s32[]{:S(2)}) async-start(), calls=%async_computation.4 | async-start | bytes 2228224
  148.1 1.0 copy-start.10
  149.2 89.9 %copy-start.11 = (s32[1,16]{1,0:T(1,128)S(1)}, s32[1,16]{1,0:T(1,128)}, u32[]{:S(2)}) copy-start(s32[1,16]{1,0:T(1,128)} %param.13) | copy-start | bytes 196
  164.1 0.7 copy-start.6
  164.8 0.7 copy-start.7
  165.4 0.7 copy-start.8
  240.1 16.0 %all-to-all-start.1 = ((f32[8,4,8,128]{3,1,2,0:T(4,128)}), f32[8,4,8,128]{3,1,2,0:T(4,128)S(1)}, u32[]{:S(2)}, u32[]{:S(2)}) async-start(f32[8,4,8,128]{3,1,2,0:T(4,128)} %copy.16), calls=%async_computation.1 | async-start | bytes 262144 | tf_op jit(solution)/shard_map/all_to_all | solution.py:359
Sparse Core Ops, SparseCore 0:
  64.8 83.3 all-reduce.2
  152.3 73.4 reduce-scatter.3

commit v2 on v1

--- a/solution.py
+++ b/solution.py
@@ -262,12 +262,84 @@
     return [jnp.concatenate(rows, 0) for rows in state]
 
 
-def factor_kernel(ps_ref, cth_ref, ctl_ref, red_ref, qi_ref, a_ref, x_ref):
+def modes_kernel(yh_ref, yl_ref, cth_ref, ctl_ref, out_ref):
+    h = yh_ref[...]
+    out_ref[...] = mm(h, cth_ref[...]) + mm(h, ctl_ref[...]) + mm(yl_ref[...], cth_ref[...])
+
+
+def modes_of(yh, yl, cth, ctl):
+    rows = yh.shape[0]
+    t = 512
+    tile = pl.BlockSpec((t, 256), lambda p: (p, 0))
+    whole = pl.BlockSpec((256, 256), lambda p: (0, 0))
+    return pl.pallas_call(
+        modes_kernel,
+        out_shape=jax.ShapeDtypeStruct((rows, 256), F32),
+        grid=(rows // t,),
+        in_specs=[tile, tile, whole, whole],
+        out_specs=tile,
+        name="modes",
+    )(yh, yl, cth, ctl)
+
+
+EARLY = 5
+
+
+def offsets(me):
+    y, z = me // 4, lax.rem(me, 4)
+    turns = ((0, 1), (1, 0), (0, 3), (3, 0), (1, 1), (3, 3), (1, 3), (3, 1),
+             (0, 2), (2, 0), (1, 2), (2, 1), (3, 2), (2, 3), (2, 2))
+    return [lax.rem(y + dy, 4) * 4 + lax.rem(z + dz, 4) for dy, dz in turns]
+
+
+def finish_kernel(owners, ps_ref, w_ref, hot_ref, cth_ref, ctl_ref, red_ref, asm_ref,
+                  ps_in, ps_all, w_in, a_ref, x_ref, cond_ref, cond_in, dense, dense_in, slab,
+                  slab_in, send_sem, recv_sem):
+    count = 16
     size = 256
+    me = lax.axis_index("blk")
+    mine = lax.axis_index("comp")
+    peers = offsets(me)
+    friends = [lax.rem(mine + d, owners) for d in range(1, owners)]
+    barrier = pltpu.get_barrier_semaphore()
+    for p in peers:
+        pl.semaphore_signal(barrier, inc=1, device_id={"blk": p}, device_id_type=MESH)
+    for f in friends:
+        pl.semaphore_signal(barrier, inc=1, device_id={"comp": f}, device_id_type=MESH)
+    pl.semaphore_wait(barrier, len(peers) + len(friends))
+
+    def copy(src, dst, phase, peer, slot, axis="blk"):
+        return pltpu.make_async_remote_copy(
+            src_ref=src, dst_ref=dst, send_sem=send_sem.at[phase, peer],
+            recv_sem=recv_sem.at[phase, slot], device_id={axis: peer}, device_id_type=MESH)
+
+    def part(p):
+        return pl.ds(pl.multiple_of(p * 16, 16), 16)
+
+    gram_out = [copy(ps_ref.at[part(p)], ps_in.at[me], 0, p, me) for p in peers]
+    w_out = [copy(w_ref.at[p], w_in.at[me], 2, p, me) for p in peers]
+    for c in gram_out:
+        c.start()
+    for c in w_out[:EARLY]:
+        c.start()
+    acc = ps_ref[part(me), :]
+    for p in peers:
+        copy(ps_ref.at[part(p)], ps_in.at[p], 0, p, p).wait_recv()
+        acc = acc + ps_in[p]
+    ps_all[part(me), :] = acc
+    own = ps_all.at[part(me)]
+    sums_out = [copy(own, own, 1, p, me) for p in peers]
+    for c in sums_out:
+        c.start()
+    for c in w_out[EARLY:]:
+        c.start()
+    for p in peers:
+        copy(own, ps_all.at[part(p)], 1, p, p).wait_recv()
+
     row = lax.broadcasted_iota(jnp.int32, (size, size), 0)
     column = lax.broadcasted_iota(jnp.int32, (size, size), 1)
     for t in range(2):
-        g = ps_ref[:, t * size:(t + 1) * size]
+        g = ps_all[:, t * size:(t + 1) * size]
         a_ref[t] = (g + g.T) * 0.5
         x_ref[t] = jnp.where(row == column, 1.0, 0.0)
     for k in range(4):
@@ -282,82 +354,92 @@
                 low = au[:, hi:].T
                 a_ref[t, hi:, :] = a_ref[t, hi:, :] - mmh(low, au)
                 x_ref[t, hi:, :] = x_ref[t, hi:, :] - mmh(low, xu)
+
+    total = w_ref[me]
+    for p in peers:
+        copy(w_ref.at[p], w_in.at[p], 2, p, p).wait_recv()
+        total = total + w_in[p]
+    scaled = mmh(x_ref[1], total)
+    cond_ref[...] = mmh(scaled.T, scaled)
+
+    def eight(p):
+        return pl.ds(pl.multiple_of(p * 8, 8), 8)
+
+    cond_out = [copy(cond_ref.at[eight(p)], cond_in.at[me], 3, p, me) for p in peers]
+    for c in cond_out:
+        c.start()
     ci = x_ref[0]
     ct = ci.T
-    red_ref[...] = mmh(mmh(ci, ps_ref[:, size:]), ct)
-    qi_ref[...] = x_ref[1]
+    red_ref[...] = mmh(mmh(ci, ps_all[:, size:]), ct)
     h, l = split(ct * 256.0)
     cth_ref[...] = h
     ctl_ref[...] = l
-
-
-def factor(ps):
+    cond_in[me] = cond_ref[eight(me), :]
+    for p in peers:
+        copy(cond_ref.at[eight(p)], cond_in.at[p], 3, p, p).wait_recv()
+    pieces = [cond_in[i] for i in range(count)]
+    for g in range(4 * owners):
+        dense[g] = sum(hot_ref[g, i] * pieces[i] for i in range(count))
+
+    def four(o):
+        return pl.ds(o * 4, 4)
+
+    dense_out = [copy(dense.at[four(f)], dense_in.at[mine], 4, f, mine, "comp") for f in friends]
+    for c in dense_out:
+        c.start()
+    acc = dense[four(mine)]
+    for f in friends:
+        copy(dense.at[four(f)], dense_in.at[f], 4, f, f, "comp").wait_recv()
+        acc = acc + dense_in[f]
+    slab[...] = acc
+    slab_out = [copy(slab, slab_in.at[me], 5, p, me) for p in peers]
+    for c in slab_out:
+        c.start()
+    asm_ref[:, eight(me), :] = acc
+    for p in peers:
+        copy(slab, slab_in.at[p], 5, p, p).wait_recv()
+        asm_ref[:, eight(p), :] = slab_in[p]
+    for c in gram_out + w_out + sums_out + cond_out + dense_out + slab_out:
+        c.wait_send()
+
+
+def finish(ps, w, hot, owners):
     sq = jax.ShapeDtypeStruct((256, 256), F32)
     sb = jax.ShapeDtypeStruct((256, 256), BF)
     vm = pl.BlockSpec(memory_space=pltpu.VMEM)
     return pl.pallas_call(
-        factor_kernel,
-        out_shape=(sb, sb, sq, sq),
-        in_specs=[vm],
+        functools.partial(finish_kernel, owners),
+        out_shape=(sb, sb, sq, jax.ShapeDtypeStruct((4, 128, 128), F32)),
+        in_specs=[vm, vm, pl.BlockSpec(memory_space=pltpu.SMEM)],
         out_specs=(vm,) * 4,
-        scratch_shapes=[pltpu.VMEM((2, 256, 256), F32)] * 2,
-        compiler_params=pltpu.CompilerParams(vmem_limit_bytes=32 * MIB),
-        cost_estimate=pl.CostEstimate(flops=4 * 10**9, bytes_accessed=10**6, transcendentals=0),
-        name="factor",
-    )(ps)
-
-
-def modes_kernel(yh_ref, yl_ref, cth_ref, ctl_ref, out_ref):
-    h = yh_ref[...]
-    out_ref[...] = mm(h, cth_ref[...]) + mm(h, ctl_ref[...]) + mm(yl_ref[...], cth_ref[...])
-
-
-def modes_of(yh, yl, cth, ctl):
-    rows = yh.shape[0]
-    t = 512
-    tile = pl.BlockSpec((t, 256), lambda p: (p, 0))
-    whole = pl.BlockSpec((256, 256), lambda p: (0, 0))
-    return pl.pallas_call(
-        modes_kernel,
-        out_shape=jax.ShapeDtypeStruct((rows, 256), F32),
-        grid=(rows // t,),
-        in_specs=[tile, tile, whole, whole],
-        out_specs=tile,
-        name="modes",
-    )(yh, yl, cth, ctl)
-
-
-def condense_kernel(qi_ref, w_ref, out_ref):
-    scaled = mmh(qi_ref[...], w_ref[...])
-    out_ref[...] = mmh(scaled.T, scaled)
-
-
-def condense(qi, w):
-    vm = pl.BlockSpec(memory_space=pltpu.VMEM)
-    return pl.pallas_call(
-        condense_kernel,
-        out_shape=jax.ShapeDtypeStruct((128, 128), F32),
-        in_specs=[vm] * 2,
-        out_specs=vm,
-        name="condense",
-    )(qi, w)
+        scratch_shapes=[
+            pltpu.VMEM((16, 16, 512), F32),
+            pltpu.VMEM((256, 512), F32),
+            pltpu.VMEM((16, 256, 128), F32),
+            pltpu.VMEM((2, 256, 256), F32),
+            pltpu.VMEM((2, 256, 256), F32),
+            pltpu.VMEM((128, 128), F32),
+            pltpu.VMEM((16, 8, 128), F32),
+            pltpu.VMEM((4 * owners, 8, 128), F32),
+            pltpu.VMEM((owners, 4, 8, 128), F32),
+            pltpu.VMEM((4, 8, 128), F32),
+            pltpu.VMEM((16, 4, 8, 128), F32),
+            pltpu.SemaphoreType.DMA((6, 16)),
+            pltpu.SemaphoreType.DMA((6, 16)),
+        ],
+        compiler_params=pltpu.CompilerParams(
+            collective_id=1, has_side_effects=True, vmem_limit_bytes=40 * MIB),
+        name="finish",
+    )(ps, w, hot)
 
 
 def local(start_modes, stiff_diag, stiff_off, mass_blocks, coupling, interface_block, global_iface):
-    count = lax.axis_size("blk")
-    yh, yl, zh, zl = chain(start_modes[0], stiff_diag[0], stiff_off[0], count)
+    owners = lax.axis_size("comp")
+    yh, yl, zh, zl = chain(start_modes[0], stiff_diag[0], stiff_off[0], lax.axis_size("blk"))
     ps, w = gram(interface_block[0], yh, yl, zh, zl, mass_blocks[0], coupling[0])
-    ps = lax.psum(ps, "blk")
-    mine = lax.psum_scatter(w, "blk", scatter_dimension=0, tiled=False)
-    cth, ctl, reduced, qi = factor(ps)
+    hot = (jnp.arange(4 * owners, dtype=jnp.int32)[:, None] == global_iface[0][None, :]).astype(F32)
+    cth, ctl, reduced, assembled = finish(ps, w, hot, owners)
     modes = modes_of(yh, yl, cth, ctl)
-    cond = condense(qi, mine)
-    pieces = lax.all_to_all(cond.reshape(count, 128 // count, 128), "blk", 0, 0, tiled=True)
-    owners = lax.axis_size("comp")
-    hot = (jnp.arange(4 * owners, dtype=jnp.int32)[:, None] == global_iface[0][None, :]).astype(F32)
-    dense = jnp.einsum("gj,jkl->gkl", hot, pieces, precision=HI)
-    slab = jnp.sum(lax.all_to_all(dense.reshape(owners, 4, 128 // count, 128), "comp", 0, 0, tiled=True), 0)
-    assembled = lax.all_gather(slab, "blk", axis=1, tiled=True)
     return modes[None], reduced[None], assembled
 
 

time: 286 us -> 137 us (0.48); the launches traced: 280 us -> 137 us
  waiting for transfers between devices: 143 us -> 0 us
  Pallas kernels: 74.8 us -> 127 us
  blocking collectives: 27.6 us -> 0 us
  between operations: 14.1 us -> 0.73 us
  starting transfers between devices: 8.46 us -> 0 us
  local copies, waits for them, and re-layouts: 12.2 us -> 9.08 us
    psum x1 -> x0, waiting for transfers between devices: 82.7 us -> none  [local(): ps = lax.psum(ps, 'blk')]
    unnamed x3 -> x0, waiting for transfers between devices: 60.2 us -> none
    pallas_call x2 -> x1, Pallas kernels: 17.3 us -> 69.9 us  [finish(): pl.pallas_call(functools.partial(finish_kernel, owners), out_shape=(sb, s...]
    all_gather x1 -> x0, blocking collectives: 16.7 us -> none  [local(): assembled = lax.all_gather(slab, 'blk', axis=1, tiled=True)]
    all_to_all x1 -> x0, blocking collectives: 10.9 us -> none  [local(): lax.all_to_all(cond.reshape(count, 128 // count, 128), 'blk', 0, 0, tiled...]
    all_to_all x1 -> x0, starting transfers between devices: 8.2 us -> none  [local(): lax.all_to_all(dense.reshape(owners, 4, 128 // count, 128), 'comp', 0, 0,...]
    unnamed x25 -> x20, local copies, waits for them, and re-layouts: 11.5 us -> 9.08 us
  transfers between devices with their start and end apart: 3 -> 0, of which waited for: 2 -> 0; matrix products, arithmetic and copies ran while one was open for 0% -> 0% of each run, Pallas kernels for 8% -> 0%
where the time goes in v2:
time: 137 us
  Pallas kernels  127 us (93%)
  local copies, waits for them, and re-layouts  9.08 us (7%)
    pallas_call x1, Pallas kernels, finish(): pl.pallas_call(functools.partial(finish_kernel, owners), out_shape=(sb, s...  69.9 us
    pallas_call x1, Pallas kernels, chain(): pl.pallas_call(functools.partial(chain_kernel, nb, count), out_shape=(out...  34.9 us
    pallas_call x1, Pallas kernels, gram(): pl.pallas_call(gram_kernel, out_shape=(jax.ShapeDtypeStruct((256, 512), F...  14.3 us
    unnamed x20, local copies, waits for them, and re-layouts  9.08 us
    pallas_call x1, Pallas kernels, modes_of(): pl.pallas_call(modes_kernel, out_shape=jax.ShapeDtypeStruct((rows, 256),...  7.77 us

profile of v2, /device:TPU:1, one launch (start us, length us, event | category | flops | bytes accessed | tf_op | source)
XLA Modules:
  0.0 136.6 jit_solution(11278680406031912003)
XLA Ops:
  0.6 0.0 copy-start.2
  0.6 0.0 copy-start.7
  0.7 34.9 %chain.1 = (bf16[4096,256]{1,0:T(8,128)(2,1)}, bf16[4096,256]{1,0:T(8,128)(2,1)}, bf16[4096,256]{1,0:T(8,128)(2,1)}, bf16[4096,256]{1,0:T(8,128)(2,1)}) custom-call(f32[4096,256]{1,0:T(8,128)} %bitcast.12, f32[32,128,128]{2,1,0:T(8,128)} %bitcast.15, f32[32,128,128]{2,1,0:T(8,128)} %bitcast.16), custom_call_target="tpu_custom_call" | custom-call | tf_op jit(solution)/shard_map/chain/pallas_call | solution.py:161
  35.6 0.0 copy-done.2
  35.6 0.0 copy-done.7
  35.6 0.0 copy-start
  35.6 1.6 %copy-done = bf16[4096,256]{1,0:T(8,128)(2,1)S(1)} copy-done((bf16[4096,256]{1,0:T(8,128)(2,1)S(1)}, bf16[4096,256]{1,0:T(8,128)(2,1)}, u32[]{:S(2)}) %copy-start) | copy-done | bytes 2097176
  37.2 0.0 copy-start.1
  37.2 1.6 %copy-done.1 = bf16[4096,256]{1,0:T(8,128)(2,1)S(1)} copy-done((bf16[4096,256]{1,0:T(8,128)(2,1)S(1)}, bf16[4096,256]{1,0:T(8,128)(2,1)}, u32[]{:S(2)}) %copy-start.1) | copy-done | bytes 2097176
  38.8 0.0 copy-start.3
  38.8 1.6 %copy-done.3 = bf16[4096,256]{1,0:T(8,128)(2,1)S(1)} copy-done((bf16[4096,256]{1,0:T(8,128)(2,1)S(1)}, bf16[4096,256]{1,0:T(8,128)(2,1)}, u32[]{:S(2)}) %copy-start.3) | copy-done | bytes 2097176
  40.4 0.0 copy-start.4
  40.4 1.6 %copy-done.4 = bf16[4096,256]{1,0:T(8,128)(2,1)S(1)} copy-done((bf16[4096,256]{1,0:T(8,128)(2,1)S(1)}, bf16[4096,256]{1,0:T(8,128)(2,1)}, u32[]{:S(2)}) %copy-start.4) | copy-done | bytes 2097176
  42.0 0.0 copy-start.8
  42.0 14.3 %gram.1 = (f32[256,512]{1,0:T(8,128)S(1)}, f32[16,256,128]{2,1,0:T(8,128)S(1)}) custom-call(s32[32]{0:T(128)S(1)} %bitcast.11, bf16[4096,256]{1,0:T(8,128)(2,1)S(1)} %copy-done, bf16[4096,256]{1,0:T(8,128)(2,1)S(1)} %copy-done.1, bf16[4096,256]{1,0:T(8,128)(2,1)S(1)} %copy-done.3, bf16[4096,256]{1,0:T(8,128)(2,1)S(1)} %copy-done.4, ...), custom_call_target="tpu_custom_call" | custom-call | tf_op jit(solution)/shard_map/gram/pallas_call | solution.py:218
  56.3 0.0 copy-done.8
  56.3 69.9 %finish.1 = (bf16[256,256]{1,0:T(8,128)(2,1)S(1)}, bf16[256,256]{1,0:T(8,128)(2,1)S(1)}, f32[256,256]{1,0:T(8,128)S(1)}, f32[4,128,128]{2,1,0:T(8,128)S(1)}) custom-call(f32[256,512]{1,0:T(8,128)S(1)} %get-tuple-element.17.ps_ref, f32[16,256,128]{2,1,0:T(8,128)S(1)} %get-tuple-element.18.w_ref, f32[32,16]{1,0:T(8,128)S(1)} %fusion.hot_ref), custom_call_target="tpu_custom_call" | custom-call | tf_op jit(solution)/shard_map/finish/pallas_call | solution.py:410
  126.2 0.0 copy-start.5
  126.2 0.6 copy-done.5
  126.8 0.0 copy-start.6
  126.8 0.7 copy-done.6
  127.5 7.8 %modes.1 = f32[4096,256]{1,0:T(8,128)} custom-call(bf16[4096,256]{1,0:T(8,128)(2,1)} %get-tuple-element.13.yh_ref, bf16[4096,256]{1,0:T(8,128)(2,1)} %get-tuple-element.14.yl_ref, bf16[256,256]{1,0:T(8,128)(2,1)} %copy-done.5, bf16[256,256]{1,0:T(8,128)(2,1)} %copy-done.6), custom_call_target="tpu_custom_call" | custom-call | tf_op jit(solution)/shard_map/modes/pallas_call | solution.py:275
  135.2 0.7 copy.12
  135.9 0.7 copy.13
  (1 shorter events, 0.0 us)
Async XLA Ops:
  0.6 35.0 %copy-start.2 = (f32[1,32,128,128]{3,2,1,0:T(8,128)S(1)}, f32[1,32,128,128]{3,2,1,0:T(8,128)}, u32[]{:S(2)}) copy-start(f32[1,32,128,128]{3,2,1,0:T(8,128)} %param.10) | copy-start | bytes 6291460
  0.6 35.0 %copy-start.7 = (s32[1,32]{1,0:T(1,128)S(1)}, s32[1,32]{1,0:T(1,128)}, u32[]{:S(2)}) copy-start(s32[1,32]{1,0:T(1,128)} %param.12) | copy-start | bytes 388
  35.6 1.6 %copy-start = (bf16[4096,256]{1,0:T(8,128)(2,1)S(1)}, bf16[4096,256]{1,0:T(8,128)(2,1)}, u32[]{:S(2)}) copy-start(bf16[4096,256]{1,0:T(8,128)(2,1)} %get-tuple-element.13.yh_ref) | copy-start | bytes 6291460
  37.2 1.6 %copy-start.1 = (bf16[4096,256]{1,0:T(8,128)(2,1)S(1)}, bf16[4096,256]{1,0:T(8,128)(2,1)}, u32[]{:S(2)}) copy-start(bf16[4096,256]{1,0:T(8,128)(2,1)} %get-tuple-element.14.yl_ref) | copy-start | bytes 6291460
  38.8 1.6 %copy-start.3 = (bf16[4096,256]{1,0:T(8,128)(2,1)S(1)}, bf16[4096,256]{1,0:T(8,128)(2,1)}, u32[]{:S(2)}) copy-start(bf16[4096,256]{1,0:T(8,128)(2,1)} %get-tuple-element.15.zh_ref) | copy-start | bytes 6291460
  40.4 1.6 %copy-start.4 = (bf16[4096,256]{1,0:T(8,128)(2,1)S(1)}, bf16[4096,256]{1,0:T(8,128)(2,1)}, u32[]{:S(2)}) copy-start(bf16[4096,256]{1,0:T(8,128)(2,1)} %get-tuple-element.16.zl_ref) | copy-start | bytes 6291460
  42.0 14.3 %copy-start.8 = (s32[1,16]{1,0:T(1,128)S(1)}, s32[1,16]{1,0:T(1,128)}, u32[]{:S(2)}) copy-start(s32[1,16]{1,0:T(1,128)} %param.13) | copy-start | bytes 196
  126.2 0.7 copy-start.5
  126.8 0.7 copy-start.6

commit v3 on v0

v3 whole, which is shorter than its diff:
```python
import functools

import jax
import jax.numpy as jnp
from jax import lax
from jax.experimental import pallas as pl
from jax.experimental.pallas import tpu as pltpu
from jax.sharding import PartitionSpec as P

BF = jnp.bfloat16
F32 = jnp.float32
STEP = 0.15
MESH = pl.DeviceIdType.MESH
HI = lax.Precision.HIGHEST
MIB = 1 << 20
NB = 32
ROWS = NB * 128
BLK = 16
COMP = 8
CHUNKS = 4
EARLY = 6


def split(x):
    hi = x.astype(BF)
    lo = (x - hi.astype(F32)).astype(BF)
    return hi, lo


def mm(a, b):
    return jnp.dot(a, b, preferred_element_type=F32)


def mmh(a, b):
    return jnp.dot(a, b, preferred_element_type=F32, precision=HI)


def cat(parts, axis):
    return jnp.concatenate(parts, axis)


def rows_at(start, size):
    return pl.ds(pl.multiple_of(start, min(size, 128)), size)


def diag_inverse(mats):
    groups = 8
    sub = lax.broadcasted_iota(jnp.int32, (8, 128), 0)
    lane = lax.broadcasted_iota(jnp.int32, (8, 128), 1)
    state = []
    for mat in mats:
        full = cat([mat, jnp.zeros_like(mat)], 1)
        state.append([
            jnp.where(lane == sub + (64 + 8 * g), 1.0, full[8 * g:8 * g + 8]) for g in range(groups)
        ])
    for k in range(groups):
        cols = [[[jnp.broadcast_to(rows[g][:, 8 * k + c:8 * k + c + 1], (8, 128)) for c in range(8)]
                 for g in range(k, groups)] for rows in state]
        for c in range(8):
            for rows, col in zip(state, cols):
                mine = col[0]
                rs = lax.rsqrt(jnp.broadcast_to(mine[c][c:c + 1, :], (8, 128)))
                u = jnp.broadcast_to(rows[k][c:c + 1, :], (8, 128)) * rs
                heads = {n: jnp.broadcast_to(mine[n][c:c + 1, :], (8, 128)) * rs for n in range(c + 1, 8)}
                for g in range(k, groups):
                    mult = col[g - k][c] * rs
                    if g == k:
                        mult = jnp.where(sub > c, mult, 0.0)
                        rows[g] = jnp.where(sub == c, u, rows[g] - mult * u)
                    else:
                        rows[g] = rows[g] - mult * u
                    for n in range(c + 1, 8):
                        col[g - k][n] = col[g - k][n] - mult * heads[n]
    return [cat(rows, 0) for rows in state]


def offsets(me):
    y, z = me // 4, lax.rem(me, 4)
    turns = ((0, 1), (1, 0), (0, 3), (3, 0), (1, 1), (3, 3), (1, 3), (3, 1),
             (0, 2), (2, 0), (1, 2), (2, 1), (3, 2), (2, 3), (2, 2))
    return [lax.rem(y + dy, 4) * 4 + lax.rem(z + dz, 4) for dy, dz in turns]


def kernel(links, hot, x_hbm, d_hbm, e_hbm, m_hbm, c_hbm, modes_ref, red_ref, asm_ref,
           x, d, e, m, cpl, xh, xl, fh, fl, yh, yl, ah, al, cum, ct,
           edge, halo, enext, gram, gram_in, sums, w, w_in, fa, fx,
           cond, cond_in, dense, dense_in, slab, slab_in,
           load_sem, halo_send, halo_recv, send_sem, recv_sem):
    me = lax.axis_index("blk")
    mine = lax.axis_index("comp")
    left, right = lax.rem(me + BLK - 1, BLK), lax.rem(me + 1, BLK)
    peers = offsets(me)
    friends = [lax.rem(mine + k, COMP) for k in range(1, COMP)]
    barrier = pltpu.get_barrier_semaphore()
    for p in peers:
        pl.semaphore_signal(barrier, inc=1, device_id={"blk": p}, device_id_type=MESH)
    for f in friends:
        pl.semaphore_signal(barrier, inc=1, device_id={"comp": f}, device_id_type=MESH)

    step = NB // CHUNKS
    loads = []
    for k in range(CHUNKS):
        b, r = pl.ds(k * step, step), pl.ds(k * step * 128, step * 128)
        trio = [pltpu.make_async_copy(e_hbm.at[b], e.at[b], load_sem.at[3 * k]),
                pltpu.make_async_copy(d_hbm.at[b], d.at[b], load_sem.at[3 * k + 1]),
                pltpu.make_async_copy(x_hbm.at[r], x.at[r], load_sem.at[3 * k + 2])]
        for t in trio:
            t.start()
        loads.append(trio)
    late = [pltpu.make_async_copy(m_hbm, m, load_sem.at[3 * CHUNKS]),
            pltpu.make_async_copy(c_hbm, cpl, load_sem.at[3 * CHUNKS + 1])]
    for t in late:
        t.start()

    has_left, has_right = me > 0, me < BLK - 1

    def put_a(b, col, block):
        hi, lo = split(block)
        ah[b, :, col * 128:(col + 1) * 128] = hi
        al[b, :, col * 128:(col + 1) * 128] = lo

    def build(b):
        link = e[b]
        put_a(b, 0, jnp.where(jnp.logical_or(has_left, b > 0), link, 0.0))
        put_a(b, 1, d[b])
        hi, lo = split(x[rows_at(b * 128, 128), :])
        xh[rows_at(b * 128 + 128, 128), :] = hi
        xl[rows_at(b * 128 + 128, 128), :] = lo
        put_a(jnp.where(b > 0, b - 1, NB - 1), 2, link.T)

    for k in range(CHUNKS):
        for t in loads[k]:
            t.wait()

        def builds(i, _, k=k):
            build(k * step + 2 * i)
            build(k * step + 2 * i + 1)
            return 0

        lax.fori_loop(0, step // 2, builds, 0)

    pl.semaphore_wait(barrier, len(peers) + len(friends))

    def send(src, dst, slot, peer):
        copy = pltpu.make_async_remote_copy(
            src_ref=src, dst_ref=dst, send_sem=halo_send.at[slot], recv_sem=halo_recv.at[slot],
            device_id={"blk": peer}, device_id_type=MESH)
        copy.start()
        return copy

    def copy(src, dst, phase, peer, slot, axis="blk"):
        return pltpu.make_async_remote_copy(
            src_ref=src, dst_ref=dst, send_sem=send_sem.at[phase, peer],
            recv_sem=recv_sem.at[phase, slot], device_id={axis: peer}, device_id_type=MESH)

    halos = [
        send(e.at[0], enext, 6, left),
        send(x.at[pl.ds(ROWS - 128, 128)], halo.at[0], 0, right),
        send(x.at[pl.ds(0, 128)], halo.at[1], 1, left),
    ]

    def product(vh, vl, p):
        out = []
        for q in range(2):
            s = rows_at(p * 256 + q * 128, 384)
            h, l, a = vh[s, :], vl[s, :], ah[2 * p + q]
            out.append(mm(cat([a, a, al[2 * p + q]], 1), cat([h, l, h], 0)))
        return cat(out, 0)

    def own(p):
        return rows_at(p * 256 + 128, 256)

    def apply_f(p):
        f = x[rows_at(p * 256, 256), :] * (1.0 / 256) - product(xh, xl, p) * (STEP / 256)
        fh[own(p), :], fl[own(p), :] = split(f)
        return f

    def apply_y(p):
        f = fh[own(p), :].astype(F32) + fl[own(p), :].astype(F32)
        y = f - product(fh, fl, p) * STEP
        yh[own(p), :], yl[own(p), :] = split(y)
        return y

    def apply_z(p):
        zh, zl = split(product(yh, yl, p))
        s = rows_at(p * 256, 256)
        th, tl = xh[s, :], xl[s, :]
        gram[1] = gram[1] + mm(cat([th, th, tl], 1), cat([zh, zl, zh], 0))

    def wait_halo(rnd, vh, vl):
        if rnd == 0:
            halos[0].wait()
            put_a(NB - 1, 2, jnp.where(has_right, enext[...], 0.0).T)
        halos[2 * rnd + 1].wait()
        vh[0:128, :], vl[0:128, :] = split(jnp.where(has_left, halo[2 * rnd], 0.0))
        halos[2 * rnd + 2].wait()
        vh[ROWS + 128:ROWS + 256, :], vl[ROWS + 128:ROWS + 256, :] = split(
            jnp.where(has_right, halo[2 * rnd + 1], 0.0))

    def pairs(fn, start, stop):
        def body(i, _):
            fn(start + 2 * i)
            fn(start + 2 * i + 1)
            return 0

        lax.fori_loop(0, (stop - start) // 2, body, 0)

    last_pair = NB // 2 - 1
    for rnd, (fn, vh, vl) in enumerate(((apply_f, xh, xl), (apply_y, fh, fl))):
        pairs(fn, 1, last_pair)
        wait_halo(rnd, vh, vl)
        edge[2 * rnd] = fn(last_pair)[128:, :]
        halos.append(send(edge.at[2 * rnd], halo.at[2 * rnd + 2], 2 * rnd + 2, right))
        edge[2 * rnd + 1] = fn(0)[:128, :]
        halos.append(send(edge.at[2 * rnd + 1], halo.at[2 * rnd + 3], 2 * rnd + 3, left))

    for t in late:
        t.wait()
    gram[...] = jnp.zeros_like(gram)
    cum[0] = jnp.zeros((256, 128), F32)

    def mass(p):
        h, l = yh[own(p), :], yl[own(p), :]
        parts = []
        for q in range(2):
            mh, ml = split(m[2 * p + q])
            s = slice(q * 128, (q + 1) * 128)
            both = mm(cat([cat([mh, mh], 1), cat([ml, ml], 1)], 0), cat([h[s], l[s]], 0))
            parts.append(both[:128] + both[128:])
        mh, ml = split(cat(parts, 0))
        th, tl = h.T, l.T
        xh[rows_at(p * 256, 256), :] = th
        xl[rows_at(p * 256, 256), :] = tl
        gram[0] = gram[0] + mm(cat([th, th, tl], 1), cat([mh, ml, mh], 0))
        for q in range(2):
            b = 2 * p + q
            ch, cl = split(cpl[b])
            cc = cat([ch, cl], 1)
            s = slice(q * 128, (q + 1) * 128)
            both = mm(cat([th[:, s], tl[:, s]], 1), cat([cc, cc], 0))
            cum[b + 1] = both[:, :128] + both[:, 128:] + cum[links[b]]

    pairs(mass, 0, NB // 2)

    def part(p):
        return rows_at(p * 16, 16)

    def reduce_out(t):
        out = [copy(gram.at[t, part(p)], gram_in.at[t, me], t, p, me) for p in peers]
        for c in out:
            c.start()
        return out

    def reduce_in(t):
        acc = gram[t, part(me), :]
        for p in peers:
            copy(gram.at[t, part(p)], gram_in.at[t, p], t, p, p).wait_recv()
            acc = acc + gram_in[t, p]
        sums[t, part(me), :] = acc
        piece = sums.at[t, part(me)]
        out = [copy(piece, piece, 2 + t, p, me) for p in peers]
        for c in out:
            c.start()
        return out

    def gathered(t):
        for p in peers:
            copy(sums.at[t, part(me)], sums.at[t, part(p)], 2 + t, p, p).wait_recv()

    started = reduce_out(0)

    def projection(j, _):
        w[j] = cum[links[NB + j]]
        return 0

    lax.fori_loop(0, BLK, projection, 0)
    w_out = [copy(w.at[p], w_in.at[me], 4, p, me) for p in peers]
    for c in w_out[:EARLY]:
        c.start()

    pairs(apply_z, 1, 9)
    started += reduce_in(0)
    pairs(apply_z, 9, last_pair)
    wait_halo(2, yh, yl)
    apply_z(0)
    apply_z(last_pair)
    started += reduce_out(1)
    started += reduce_in(1)
    for c in w_out[EARLY:]:
        c.start()
    gathered(0)
    gathered(1)

    size = 256
    row = lax.broadcasted_iota(jnp.int32, (size, size), 0)
    column = lax.broadcasted_iota(jnp.int32, (size, size), 1)
    for t in range(2):
        g = sums[t]
        fa[t] = (g + g.T) * 0.5
        fx[t] = jnp.where(row == column, 1.0, 0.0)
    for k in range(4):
        lo, hi = 64 * k, 64 * (k + 1)
        inv = diag_inverse([fa[t, lo:hi, lo:hi] for t in range(2)])
        for t in range(2):
            tri = inv[t][:, 64:]
            xu = mmh(tri, fx[t, lo:hi, :])
            fx[t, lo:hi, :] = xu
            if k < 3:
                au = mmh(tri, fa[t, lo:hi, :])
                low = au[:, hi:].T
                fa[t, hi:, :] = fa[t, hi:, :] - mmh(low, au)
                fx[t, hi:, :] = fx[t, hi:, :] - mmh(low, xu)

    total = w[me]
    for p in peers:
        copy(w.at[p], w_in.at[p], 4, p, p).wait_recv()
        total = total + w_in[p]
    scaled = mmh(fx[1], total)
    cond[...] = mmh(scaled.T, scaled)

    def eight(p):
        return rows_at(p * 8, 8)

    cond_out = [copy(cond.at[eight(p)], cond_in.at[me], 5, p, me) for p in peers]
    for c in cond_out:
        c.start()

    def modes(p):
        h, l = yh[own(p), :], yl[own(p), :]
        modes_ref[rows_at(p * 256, 256), :] = mm(cat([h, h, l], 1), ct[...])

    inverse = fx[0]
    turned = inverse.T
    red_ref[...] = mmh(mmh(inverse, sums[1]), turned)
    h, l = split(turned * 256.0)
    ct[...] = cat([h, l, h], 0)
    pairs(modes, 0, 4)
    cond_in[me] = cond[eight(me), :]
    for p in peers:
        copy(cond.at[eight(p)], cond_in.at[p], 5, p, p).wait_recv()
    pieces = [cond_in[i] for i in range(BLK)]
    for g in range(4 * COMP):
        dense[g] = sum(hot[g, i] * pieces[i] for i in range(BLK))

    def four(o):
        return pl.ds(o * 4, 4)

    dense_out = [copy(dense.at[four(f)], dense_in.at[mine], 6, f, mine, "comp") for f in friends]
    for c in dense_out:
        c.start()
    pairs(modes, 4, 10)
    acc = dense[four(mine)]
    for f in friends:
        copy(dense.at[four(f)], dense_in.at[f], 6, f, f, "comp").wait_recv()
        acc = acc + dense_in[f]
    slab[...] = acc
    slab_out = [copy(slab, slab_in.at[me], 7, p, me) for p in peers]
    for c in slab_out:
        c.start()
    asm_ref[:, eight(me), :] = acc
    pairs(modes, 10, 16)
    for p in peers:
        copy(slab, slab_in.at[p], 7, p, p).wait_recv()
        asm_ref[:, eight(p), :] = slab_in[p]
    for c in started + w_out + cond_out + dense_out + slab_out:
        c.wait_send()


def local(start_modes, stiff_diag, stiff_off, mass_blocks, coupling, interface_block, global_iface):
    ids = interface_block[0]
    order = jnp.arange(NB, dtype=jnp.int32)
    earlier = (ids[:, None] == ids[None, :]) & (order[None, :] < order[:, None])
    ends = jnp.arange(BLK, dtype=jnp.int32)[:, None] == ids[None, :]
    links = jnp.max(jnp.where(jnp.concatenate([earlier, ends], 0), order[None, :] + 1, 0), axis=1)
    hot = (jnp.arange(4 * COMP, dtype=jnp.int32)[:, None] == global_iface[0][None, :]).astype(F32)
    smem = pl.BlockSpec(memory_space=pltpu.SMEM)
    anym = pl.BlockSpec(memory_space=pl.ANY)
    vm = pl.BlockSpec(memory_space=pltpu.VMEM)
    ext = pltpu.VMEM((ROWS + 256, 256), BF)
    blocks = pltpu.VMEM((NB, 128, 128), F32)
    modes, reduced, assembled = pl.pallas_call(
        kernel,
        out_shape=(jax.ShapeDtypeStruct((ROWS, 256), F32),
                   jax.ShapeDtypeStruct((256, 256), F32),
                   jax.ShapeDtypeStruct((4, 128, 128), F32)),
        in_specs=[smem, smem] + [anym] * 5,
        out_specs=(vm,) * 3,
        scratch_shapes=[
            pltpu.VMEM((ROWS, 256), F32), blocks, blocks, blocks, blocks,
            ext, ext, ext, ext, ext, ext,
            pltpu.VMEM((NB, 128, 384), BF), pltpu.VMEM((NB, 128, 384), BF),
            pltpu.VMEM((NB + 1, 256, 128), F32),
            pltpu.VMEM((768, 256), BF),
            pltpu.VMEM((4, 128, 256), F32),
            pltpu.VMEM((6, 128, 256), F32),
            pltpu.VMEM((128, 128), F32),
            pltpu.VMEM((2, 256, 256), F32),
            pltpu.VMEM((2, BLK, 16, 256), F32),
            pltpu.VMEM((2, 256, 256), F32),
            pltpu.VMEM((BLK, 256, 128), F32),
            pltpu.VMEM((BLK, 256, 128), F32),
            pltpu.VMEM((2, 256, 256), F32),
            pltpu.VMEM((2, 256, 256), F32),
            pltpu.VMEM((128, 128), F32),
            pltpu.VMEM((BLK, 8, 128), F32),
            pltpu.VMEM((4 * COMP, 8, 128), F32),
            pltpu.VMEM((COMP, 4, 8, 128), F32),
            pltpu.VMEM((4, 8, 128), F32),
            pltpu.VMEM((BLK, 4, 8, 128), F32),
            pltpu.SemaphoreType.DMA((3 * CHUNKS + 2,)),
            pltpu.SemaphoreType.DMA((7,)),
            pltpu.SemaphoreType.DMA((7,)),
            pltpu.SemaphoreType.DMA((8, 16)),
            pltpu.SemaphoreType.DMA((8, 16)),
        ],
        compiler_params=pltpu.CompilerParams(
            collective_id=0, has_side_effects=True, vmem_limit_bytes=60 * MIB),
        name="superelement",
    )(links, hot, start_modes[0], stiff_diag[0], stiff_off[0], mass_blocks[0], coupling[0])
    return modes[None], reduced[None], assembled


def solution(mesh):
    in_specs = (
        P("comp", "blk", None),
        P("comp", "blk", None, None),
        P("comp", "blk", None, None),
        P("comp", "blk", None, None),
        P("comp", "blk", None, None),
        P("comp", "blk"),
        P("comp", None),
    )
    out_specs = (P("comp", "blk", None), P("comp", None, None), P("comp", None, None))
    return jax.shard_map(local, mesh=mesh, in_specs=in_specs, out_specs=out_specs, check_vma=False)
```

time: 483 us -> 104 us (0.22); the launches traced: 478 us -> 104 us
  other arithmetic: 181 us -> 3.41 us
  matrix products: 132 us -> 0 us
  Pallas kernels: 0 us -> 94.2 us
  blocking collectives: 53.6 us -> 0 us
  starting transfers between devices: 46.8 us -> 0 us
  waiting for transfers between devices: 27 us -> 0 us
  local copies, waits for them, and re-layouts: 31.5 us -> 5.94 us
  between operations: 5.56 us -> 0.66 us
    another operation x27 -> x0, other arithmetic: 163 us -> none  [the longest x20 103 us: lower_inverse(): factor = jnp.linalg.cholesky(matrix)]
    dot_general x25 -> x0, matrix products: 128 us -> none  [the longest x8 43.7 us: block_product(): return jnp.einsum('bij,bjm->bim', blocks, vectors, precision=highest)]
    pallas_call x0 -> x1, Pallas kernels: none -> 94.2 us  [local(): pl.pallas_call(kernel, out_shape=(jax.ShapeDtypeStruct((ROWS, 256), F32),...]
    all_to_all x2 -> x0, blocking collectives: 53.6 us -> none  [sent_and_summed(): pieces = lax.all_to_all(split_up(array, dim, peers), axis, 0, 0, tiled=True)]
    all_to_all x5 -> x0, starting transfers between devices: 29.7 us -> none  [the longest x2 15.3 us: sent_and_summed(): pieces = lax.all_to_all(split_up(array, dim, peers), axis, 0, 0, tiled=True)]
    all_to_all x5 -> x0, waiting for transfers between devices: 27 us -> none  [the longest x3 17.8 us: copy_for_each(): return lax.all_to_all(copies, axis, split_axis=0, concat_axis=0, tiled=True)]
    ppermute x7 -> x0, starting transfers between devices: 17.1 us -> none  [the longest x3 11.4 us: extended_2(): lax.ppermute(lax.slice_in_dim(block, block.shape[dim] - width, None, axis...]
    concatenate x5 -> x0, other arithmetic: 12.7 us -> none  [the longest x3 12.6 us: extended_2(): block = jnp.concatenate([low, block, high], axis=dim)]
  transfers between devices with their start and end apart: 12 -> 0, of which waited for: 3 -> 0; matrix products, arithmetic and copies ran while one was open for 21% -> 0% of each run, Pallas kernels for 0% -> 0%
where the time goes in v3:
time: 104 us
  Pallas kernels  94.2 us (91%)
  local copies, waits for them, and re-layouts  5.94 us (6%)
  other arithmetic  3.41 us (3%)
    pallas_call x1, Pallas kernels, local(): pl.pallas_call(kernel, out_shape=(jax.ShapeDtypeStruct((ROWS, 256), F32),...  94.2 us
    unnamed x7, local copies, waits for them, and re-layouts  5.94 us

profile of v3, /device:TPU:1, one launch (start us, length us, event | category | flops | bytes accessed | tf_op | source)
XLA Modules:
  0.0 104.2 jit_solution(15725417077142155880)
XLA Ops:
  0.6 0.7 iota_compare_fusion.1
  1.4 0.8 fusion
  2.2 0.6 select_reduce_fusion.links
  2.8 1.3 %fusion.1.hot = f32[32,16]{1,0:T(8,128)} fusion(s32[16]{0:T(128)} %bitcast.18), kind=kLoop, calls=%fused_computation.5 | loop fusion | flops 1024 | bytes 2112 | tf_op jit(solution)/shard_map/convert_element_type | solution.py:375
  4.0 94.2 %superelement.1 = (f32[4096,256]{1,0:T(8,128)}, f32[256,256]{1,0:T(8,128)}, f32[4,128,128]{2,1,0:T(8,128)}) custom-call(s32[48]{0:T(128)} %select_reduce_fusion.links, f32[32,16]{1,0:T(8,128)} %fusion.1.hot, f32[4096,256]{1,0:T(8,128)} %bitcast.9, f32[32,128,128]{2,1,0:T(8,128)} %bitcast.11, f32[32,128,128]{2,1,0:T(8,128)} %bitcast.12, ...), custom_call_target="tpu_custom_call" | custom-call | tf_op jit(solution)/shard_map/superelement/pallas_call | solution.py:381
  98.2 0.0 copy-start.1
  98.2 0.0 copy-start
  98.2 4.5 %copy.13 = f32[1,4096,256]{2,1,0:T(8,128)} copy(f32[1,4096,256]{2,1,0:T(8,128)} %bitcast.10) | data formatting | bytes 8388608
  102.8 0.0 copy-done.1
  102.8 0.7 copy.14
  103.5 0.0 copy-done
  103.5 0.7 copy.15
  (1 shorter events, 0.0 us)
Async XLA Ops:
  98.2 4.5 %copy-start.1 = (f32[256,256]{1,0:T(8,128)S(1)}, f32[256,256]{1,0:T(8,128)}, u32[]{:S(2)}) copy-start(f32[256,256]{1,0:T(8,128)} %get-tuple-element.7) | copy-start | bytes 786436
  98.2 5.2 %copy-start = (f32[4,128,128]{2,1,0:T(8,128)S(1)}, f32[4,128,128]{2,1,0:T(8,128)}, u32[]{:S(2)}) copy-start(f32[4,128,128]{2,1,0:T(8,128)} %get-tuple-element.14) | copy-start | bytes 786436

commit v4 on v3

--- a/solution.py
+++ b/solution.py
@@ -81,8 +81,8 @@
     return [lax.rem(y + dy, 4) * 4 + lax.rem(z + dz, 4) for dy, dz in turns]
 
 
-def kernel(links, hot, x_hbm, d_hbm, e_hbm, m_hbm, c_hbm, modes_ref, red_ref, asm_ref,
-           x, d, e, m, cpl, xh, xl, fh, fl, yh, yl, ah, al, cum, ct,
+def kernel(ids, owned, x_hbm, d_hbm, e_hbm, m_hbm, c_hbm, yh, yl, ct, red_ref, asm_ref,
+           x, d, e, m, cpl, xh, xl, fh, fl, ah, al, cum,
            edge, halo, enext, gram, gram_in, sums, w, w_in, fa, fx,
            cond, cond_in, dense, dense_in, slab, slab_in,
            load_sem, halo_send, halo_recv, send_sem, recv_sem):
@@ -128,19 +128,6 @@
         xl[rows_at(b * 128 + 128, 128), :] = lo
         put_a(jnp.where(b > 0, b - 1, NB - 1), 2, link.T)
 
-    for k in range(CHUNKS):
-        for t in loads[k]:
-            t.wait()
-
-        def builds(i, _, k=k):
-            build(k * step + 2 * i)
-            build(k * step + 2 * i + 1)
-            return 0
-
-        lax.fori_loop(0, step // 2, builds, 0)
-
-    pl.semaphore_wait(barrier, len(peers) + len(friends))
-
     def send(src, dst, slot, peer):
         copy = pltpu.make_async_remote_copy(
             src_ref=src, dst_ref=dst, send_sem=halo_send.at[slot], recv_sem=halo_recv.at[slot],
@@ -152,12 +139,6 @@
         return pltpu.make_async_remote_copy(
             src_ref=src, dst_ref=dst, send_sem=send_sem.at[phase, peer],
             recv_sem=recv_sem.at[phase, slot], device_id={axis: peer}, device_id_type=MESH)
-
-    halos = [
-        send(e.at[0], enext, 6, left),
-        send(x.at[pl.ds(ROWS - 128, 128)], halo.at[0], 0, right),
-        send(x.at[pl.ds(0, 128)], halo.at[1], 1, left),
-    ]
 
     def product(vh, vl, p):
         out = []
@@ -206,8 +187,39 @@
         lax.fori_loop(0, (stop - start) // 2, body, 0)
 
     last_pair = NB // 2 - 1
+    for k in range(CHUNKS):
+        for t in loads[k]:
+            t.wait()
+        if k == 2:
+            pl.semaphore_wait(barrier, len(peers) + len(friends))
+            halos = [
+                send(e_hbm.at[0], enext, 6, left),
+                send(x_hbm.at[pl.ds(ROWS - 128, 128)], halo.at[0], 0, right),
+                send(x_hbm.at[pl.ds(0, 128)], halo.at[1], 1, left),
+            ]
+        first = k * step // 2
+        if k == 0:
+            for p in range(3):
+                build(2 * p)
+                build(2 * p + 1)
+            apply_f(1)
+            build(6)
+            build(7)
+        else:
+            def both(i, _, first=first):
+                for u in range(2):
+                    p = first + 2 * i + u
+                    apply_f(p - 2)
+                    build(2 * p)
+                    build(2 * p + 1)
+                return 0
+
+            lax.fori_loop(0, step // 4, both, 0)
+    apply_f(last_pair - 1)
+
     for rnd, (fn, vh, vl) in enumerate(((apply_f, xh, xl), (apply_y, fh, fl))):
-        pairs(fn, 1, last_pair)
+        if rnd:
+            pairs(fn, 1, last_pair)
         wait_halo(rnd, vh, vl)
         edge[2 * rnd] = fn(last_pair)[128:, :]
         halos.append(send(edge.at[2 * rnd], halo.at[2 * rnd + 2], 2 * rnd + 2, right))
@@ -218,6 +230,18 @@
         t.wait()
     gram[...] = jnp.zeros_like(gram)
     cum[0] = jnp.zeros((256, 128), F32)
+
+    def before(b):
+        slot = 0
+        for q in range(NB):
+            slot = jnp.where(jnp.logical_and(ids[q] == ids[b], q < b), q + 1, slot)
+        return slot
+
+    def final(j):
+        slot = 0
+        for q in range(NB):
+            slot = jnp.where(ids[q] == j, q + 1, slot)
+        return slot
 
     def mass(p):
         h, l = yh[own(p), :], yl[own(p), :]
@@ -238,7 +262,7 @@
             cc = cat([ch, cl], 1)
             s = slice(q * 128, (q + 1) * 128)
             both = mm(cat([th[:, s], tl[:, s]], 1), cat([cc, cc], 0))
-            cum[b + 1] = both[:, :128] + both[:, 128:] + cum[links[b]]
+            cum[b + 1] = both[:, :128] + both[:, 128:] + cum[before(b)]
 
     pairs(mass, 0, NB // 2)
 
@@ -270,7 +294,7 @@
     started = reduce_out(0)
 
     def projection(j, _):
-        w[j] = cum[links[NB + j]]
+        w[j] = cum[final(j)]
         return 0
 
     lax.fori_loop(0, BLK, projection, 0)
@@ -278,9 +302,8 @@
     for c in w_out[:EARLY]:
         c.start()
 
-    pairs(apply_z, 1, 9)
+    pairs(apply_z, 1, last_pair)
     started += reduce_in(0)
-    pairs(apply_z, 9, last_pair)
     wait_halo(2, yh, yl)
     apply_z(0)
     apply_z(last_pair)
@@ -325,22 +348,17 @@
     for c in cond_out:
         c.start()
 
-    def modes(p):
-        h, l = yh[own(p), :], yl[own(p), :]
-        modes_ref[rows_at(p * 256, 256), :] = mm(cat([h, h, l], 1), ct[...])
-
     inverse = fx[0]
     turned = inverse.T
     red_ref[...] = mmh(mmh(inverse, sums[1]), turned)
     h, l = split(turned * 256.0)
     ct[...] = cat([h, l, h], 0)
-    pairs(modes, 0, 4)
     cond_in[me] = cond[eight(me), :]
     for p in peers:
         copy(cond.at[eight(p)], cond_in.at[p], 5, p, p).wait_recv()
     pieces = [cond_in[i] for i in range(BLK)]
     for g in range(4 * COMP):
-        dense[g] = sum(hot[g, i] * pieces[i] for i in range(BLK))
+        dense[g] = sum(jnp.where(owned[i] == g, 1.0, 0.0) * pieces[i] for i in range(BLK))
 
     def four(o):
         return pl.ds(o * 4, 4)
@@ -348,7 +366,6 @@
     dense_out = [copy(dense.at[four(f)], dense_in.at[mine], 6, f, mine, "comp") for f in friends]
     for c in dense_out:
         c.start()
-    pairs(modes, 4, 10)
     acc = dense[four(mine)]
     for f in friends:
         copy(dense.at[four(f)], dense_in.at[f], 6, f, f, "comp").wait_recv()
@@ -358,7 +375,6 @@
     for c in slab_out:
         c.start()
     asm_ref[:, eight(me), :] = acc
-    pairs(modes, 10, 16)
     for p in peers:
         copy(slab, slab_in.at[p], 7, p, p).wait_recv()
         asm_ref[:, eight(p), :] = slab_in[p]
@@ -366,31 +382,45 @@
         c.wait_send()
 
 
+def result_kernel(yh, yl, ct, red, asm, modes_ref, red_ref, asm_ref, sem):
+    i = pl.program_id(0)
+    tile = modes_ref.shape[0]
+    moves = [pltpu.make_async_copy(red, red_ref, sem.at[0]), pltpu.make_async_copy(asm, asm_ref, sem.at[1])]
+
+    @pl.when(i == 0)
+    def _():
+        for t in moves:
+            t.start()
+
+    for q in range(tile // 256):
+        s = rows_at(i * tile + q * 256 + 128, 256)
+        h = yh[s, :]
+        modes_ref[q * 256:(q + 1) * 256, :] = mm(cat([h, h, yl[s, :]], 1), ct[...])
+
+    @pl.when(i == pl.num_programs(0) - 1)
+    def _():
+        for t in moves:
+            t.wait()
+
+
 def local(start_modes, stiff_diag, stiff_off, mass_blocks, coupling, interface_block, global_iface):
-    ids = interface_block[0]
-    order = jnp.arange(NB, dtype=jnp.int32)
-    earlier = (ids[:, None] == ids[None, :]) & (order[None, :] < order[:, None])
-    ends = jnp.arange(BLK, dtype=jnp.int32)[:, None] == ids[None, :]
-    links = jnp.max(jnp.where(jnp.concatenate([earlier, ends], 0), order[None, :] + 1, 0), axis=1)
-    hot = (jnp.arange(4 * COMP, dtype=jnp.int32)[:, None] == global_iface[0][None, :]).astype(F32)
     smem = pl.BlockSpec(memory_space=pltpu.SMEM)
+    hbm = pl.BlockSpec(memory_space=pltpu.HBM)
     anym = pl.BlockSpec(memory_space=pl.ANY)
     vm = pl.BlockSpec(memory_space=pltpu.VMEM)
     ext = pltpu.VMEM((ROWS + 256, 256), BF)
     blocks = pltpu.VMEM((NB, 128, 128), F32)
-    modes, reduced, assembled = pl.pallas_call(
+    yh, yl, ct, reduced, assembled = pl.pallas_call(
         kernel,
-        out_shape=(jax.ShapeDtypeStruct((ROWS, 256), F32),
-                   jax.ShapeDtypeStruct((256, 256), F32),
-                   jax.ShapeDtypeStruct((4, 128, 128), F32)),
-        in_specs=[smem, smem] + [anym] * 5,
-        out_specs=(vm,) * 3,
+        out_shape=(ext, ext, pltpu.VMEM((768, 256), BF), pltpu.VMEM((256, 256), F32),
+                   pltpu.VMEM((4, 128, 128), F32)),
+        in_specs=[smem, smem] + [hbm] * 5,
+        out_specs=(vm,) * 5,
         scratch_shapes=[
             pltpu.VMEM((ROWS, 256), F32), blocks, blocks, blocks, blocks,
-            ext, ext, ext, ext, ext, ext,
+            ext, ext, ext, ext,
             pltpu.VMEM((NB, 128, 384), BF), pltpu.VMEM((NB, 128, 384), BF),
             pltpu.VMEM((NB + 1, 256, 128), F32),
-            pltpu.VMEM((768, 256), BF),
             pltpu.VMEM((4, 128, 256), F32),
             pltpu.VMEM((6, 128, 256), F32),
             pltpu.VMEM((128, 128), F32),
@@ -414,9 +444,23 @@
             pltpu.SemaphoreType.DMA((8, 16)),
         ],
         compiler_params=pltpu.CompilerParams(
-            collective_id=0, has_side_effects=True, vmem_limit_bytes=60 * MIB),
+            collective_id=0, has_side_effects=True, vmem_limit_bytes=48 * MIB),
         name="superelement",
-    )(links, hot, start_modes[0], stiff_diag[0], stiff_off[0], mass_blocks[0], coupling[0])
+    )(interface_block[0], global_iface[0], start_modes[0], stiff_diag[0], stiff_off[0],
+      mass_blocks[0], coupling[0])
+    tile = 512
+    modes, reduced, assembled = pl.pallas_call(
+        result_kernel,
+        out_shape=(jax.ShapeDtypeStruct((ROWS, 256), F32),
+                   jax.ShapeDtypeStruct((256, 256), F32),
+                   jax.ShapeDtypeStruct((4, 128, 128), F32)),
+        grid=(ROWS // tile,),
+        in_specs=[vm] * 5,
+        out_specs=(pl.BlockSpec((tile, 256), lambda i: (i, 0)), anym, anym),
+        scratch_shapes=[pltpu.SemaphoreType.DMA((2,))],
+        compiler_params=pltpu.CompilerParams(vmem_limit_bytes=12 * MIB),
+        name="result",
+    )(yh, yl, ct, reduced, assembled)
     return modes[None], reduced[None], assembled
 
 

time: 104 us -> 105 us (level)
  Pallas kernels: 94.2 us -> 103 us
  local copies, waits for them, and re-layouts: 5.94 us -> 1.3 us
  other arithmetic: 3.41 us -> 0 us
    pallas_call x1 -> x2, Pallas kernels: 94.2 us -> 103 us  [the longest x1 97.6 us: local(): pl.pallas_call(kernel, out_shape=(ext, ext, pltpu.VMEM((768, 256), BF), p...]
    unnamed x7 -> x4, local copies, waits for them, and re-layouts: 5.94 us -> 1.3 us
    convert_element_type x1 -> x0, other arithmetic: 1.26 us -> none  [local(): (jnp.arange(4 * COMP, dtype=jnp.int32)[:, None] == global_iface[0][None,...]
where the time goes in v4:
time: 105 us
  Pallas kernels  103 us (98%)
  local copies, waits for them, and re-layouts  1.3 us (1%)
    pallas_call x1, Pallas kernels, local(): pl.pallas_call(kernel, out_shape=(ext, ext, pltpu.VMEM((768, 256), BF), p...  97.6 us
    pallas_call x1, Pallas kernels, local(): pl.pallas_call(result_kernel, out_shape=(jax.ShapeDtypeStruct((ROWS, 256)...  5.07 us

profile of v4, /device:TPU:1, one launch (start us, length us, event | category | flops | bytes accessed | tf_op | source)
XLA Modules:
  0.0 104.8 jit_solution(6604110619472757712)
XLA Ops:
  0.6 0.0 copy-start
  0.6 0.6 copy-done
  1.3 0.0 copy-start.1
  1.3 0.7 copy-done.1
  1.9 97.6 %superelement.1 = (bf16[4352,256]{1,0:T(8,128)(2,1)S(1)}, bf16[4352,256]{1,0:T(8,128)(2,1)S(1)}, bf16[768,256]{1,0:T(8,128)(2,1)S(1)}, f32[256,256]{1,0:T(8,128)S(1)}, f32[4,128,128]{2,1,0:T(8,128)S(1)}) custom-call(s32[32]{0:T(128)S(1)} %bitcast.9, s32[16]{0:T(128)S(1)} %bitcast.10, f32[4096,256]{1,0:T(8,128)} %bitcast.11, f32[32,128,128]{2,1,0:T(8,128)} %bitcast.12, ...), custom_call_target="tpu_custom_call" | custom-call | tf_op jit(solution)/shard_map/superelement/pallas_call | solution.py:413
  99.6 5.1 %result.1 = (f32[4096,256]{1,0:T(8,128)}, f32[256,256]{1,0:T(8,128)}, f32[4,128,128]{2,1,0:T(8,128)}) custom-call(bf16[4352,256]{1,0:T(8,128)(2,1)S(1)} %get-tuple-element.11.yh, bf16[4352,256]{1,0:T(8,128)(2,1)S(1)} %get-tuple-element.12.yl, bf16[768,256]{1,0:T(8,128)(2,1)S(1)} %get-tuple-element.13.ct, f32[256,256]{1,0:T(8,128)S(1)} %get-tuple-element.14.red, ...), custom_call_target="tpu_custom_call" | custom-call | tf_op jit(solution)/shard_map/result/pallas_call | solution.py:452
Async XLA Ops:
  0.6 0.7 copy-start
  1.3 0.7 copy-start.1

commit v5 on v4

--- a/solution.py
+++ b/solution.py
@@ -18,6 +18,7 @@
 BLK = 16
 COMP = 8
 CHUNKS = 4
+PARTS = 8
 EARLY = 6
 
 
@@ -81,8 +82,8 @@
     return [lax.rem(y + dy, 4) * 4 + lax.rem(z + dz, 4) for dy, dz in turns]
 
 
-def kernel(ids, owned, x_hbm, d_hbm, e_hbm, m_hbm, c_hbm, yh, yl, ct, red_ref, asm_ref,
-           x, d, e, m, cpl, xh, xl, fh, fl, ah, al, cum,
+def kernel(ids_hbm, owned_hbm, x_hbm, d_hbm, e_hbm, m_hbm, c_hbm, modes_ref, red_ref, asm_ref,
+           ids, owned, x, d, e, m, cpl, xh, xl, fh, fl, yh, yl, ah, al, cum, ct,
            edge, halo, enext, gram, gram_in, sums, w, w_in, fa, fx,
            cond, cond_in, dense, dense_in, slab, slab_in,
            load_sem, halo_send, halo_recv, send_sem, recv_sem):
@@ -108,9 +109,9 @@
             t.start()
         loads.append(trio)
     late = [pltpu.make_async_copy(m_hbm, m, load_sem.at[3 * CHUNKS]),
-            pltpu.make_async_copy(c_hbm, cpl, load_sem.at[3 * CHUNKS + 1])]
-    for t in late:
-        t.start()
+            pltpu.make_async_copy(c_hbm, cpl, load_sem.at[3 * CHUNKS + 1]),
+            pltpu.make_async_copy(ids_hbm, ids, load_sem.at[3 * CHUNKS + 2]),
+            pltpu.make_async_copy(owned_hbm, owned, load_sem.at[3 * CHUNKS + 3])]
 
     has_left, has_right = me > 0, me < BLK - 1
 
@@ -191,6 +192,8 @@
         for t in loads[k]:
             t.wait()
         if k == 2:
+            for t in late:
+                t.start()
             pl.semaphore_wait(barrier, len(peers) + len(friends))
             halos = [
                 send(e_hbm.at[0], enext, 6, left),
@@ -302,8 +305,9 @@
     for c in w_out[:EARLY]:
         c.start()
 
-    pairs(apply_z, 1, last_pair)
+    pairs(apply_z, 1, 11)
     started += reduce_in(0)
+    pairs(apply_z, 11, last_pair)
     wait_halo(2, yh, yl)
     apply_z(0)
     apply_z(last_pair)
@@ -348,17 +352,23 @@
     for c in cond_out:
         c.start()
 
+    def modes(p):
+        h, l = yh[own(p), :], yl[own(p), :]
+        modes_ref[rows_at(p * 256, 256), :] = mm(cat([h, h, l], 1), ct[...])
+
     inverse = fx[0]
     turned = inverse.T
     red_ref[...] = mmh(mmh(inverse, sums[1]), turned)
     h, l = split(turned * 256.0)
     ct[...] = cat([h, l, h], 0)
+    pairs(modes, 0, 4)
     cond_in[me] = cond[eight(me), :]
     for p in peers:
         copy(cond.at[eight(p)], cond_in.at[p], 5, p, p).wait_recv()
     pieces = [cond_in[i] for i in range(BLK)]
+    goals = [jnp.full((8, 128), owned[i], jnp.int32) for i in range(BLK)]
     for g in range(4 * COMP):
-        dense[g] = sum(jnp.where(owned[i] == g, 1.0, 0.0) * pieces[i] for i in range(BLK))
+        dense[g] = sum(jnp.where(goals[i] == g, pieces[i], 0.0) for i in range(BLK))
 
     def four(o):
         return pl.ds(o * 4, 4)
@@ -366,6 +376,7 @@
     dense_out = [copy(dense.at[four(f)], dense_in.at[mine], 6, f, mine, "comp") for f in friends]
     for c in dense_out:
         c.start()
+    pairs(modes, 4, 10)
     acc = dense[four(mine)]
     for f in friends:
         copy(dense.at[four(f)], dense_in.at[f], 6, f, f, "comp").wait_recv()
@@ -375,6 +386,7 @@
     for c in slab_out:
         c.start()
     asm_ref[:, eight(me), :] = acc
+    pairs(modes, 10, 16)
     for p in peers:
         copy(slab, slab_in.at[p], 7, p, p).wait_recv()
         asm_ref[:, eight(p), :] = slab_in[p]
@@ -382,45 +394,38 @@
         c.wait_send()
 
 
-def result_kernel(yh, yl, ct, red, asm, modes_ref, red_ref, asm_ref, sem):
-    i = pl.program_id(0)
-    tile = modes_ref.shape[0]
-    moves = [pltpu.make_async_copy(red, red_ref, sem.at[0]), pltpu.make_async_copy(asm, asm_ref, sem.at[1])]
-
-    @pl.when(i == 0)
-    def _():
-        for t in moves:
-            t.start()
-
-    for q in range(tile // 256):
-        s = rows_at(i * tile + q * 256 + 128, 256)
-        h = yh[s, :]
-        modes_ref[q * 256:(q + 1) * 256, :] = mm(cat([h, h, yl[s, :]], 1), ct[...])
-
-    @pl.when(i == pl.num_programs(0) - 1)
-    def _():
-        for t in moves:
-            t.wait()
+def result_kernel(*refs):
+    modes, red, asm, modes_out, red_out, asm_out, sem = refs
+    part = ROWS // PARTS
+    moves = [pltpu.make_async_copy(red, red_out, sem.at[PARTS]),
+             pltpu.make_async_copy(asm, asm_out, sem.at[PARTS + 1])]
+    for i in range(PARTS):
+        r = pl.ds(i * part, part)
+        moves.append(pltpu.make_async_copy(modes.at[r], modes_out.at[r], sem.at[i]))
+    for t in moves:
+        t.start()
+    for t in moves:
+        t.wait()
 
 
 def local(start_modes, stiff_diag, stiff_off, mass_blocks, coupling, interface_block, global_iface):
-    smem = pl.BlockSpec(memory_space=pltpu.SMEM)
     hbm = pl.BlockSpec(memory_space=pltpu.HBM)
-    anym = pl.BlockSpec(memory_space=pl.ANY)
     vm = pl.BlockSpec(memory_space=pltpu.VMEM)
     ext = pltpu.VMEM((ROWS + 256, 256), BF)
     blocks = pltpu.VMEM((NB, 128, 128), F32)
-    yh, yl, ct, reduced, assembled = pl.pallas_call(
+    results = pl.pallas_call(
         kernel,
-        out_shape=(ext, ext, pltpu.VMEM((768, 256), BF), pltpu.VMEM((256, 256), F32),
+        out_shape=(pltpu.VMEM((ROWS, 256), F32), pltpu.VMEM((256, 256), F32),
                    pltpu.VMEM((4, 128, 128), F32)),
-        in_specs=[smem, smem] + [hbm] * 5,
-        out_specs=(vm,) * 5,
+        in_specs=[hbm] * 7,
+        out_specs=(vm,) * 3,
         scratch_shapes=[
+            pltpu.SMEM((NB,), jnp.int32), pltpu.SMEM((BLK,), jnp.int32),
             pltpu.VMEM((ROWS, 256), F32), blocks, blocks, blocks, blocks,
-            ext, ext, ext, ext,
+            ext, ext, ext, ext, ext, ext,
             pltpu.VMEM((NB, 128, 384), BF), pltpu.VMEM((NB, 128, 384), BF),
             pltpu.VMEM((NB + 1, 256, 128), F32),
+            pltpu.VMEM((768, 256), BF),
             pltpu.VMEM((4, 128, 256), F32),
             pltpu.VMEM((6, 128, 256), F32),
             pltpu.VMEM((128, 128), F32),
@@ -437,30 +442,28 @@
             pltpu.VMEM((COMP, 4, 8, 128), F32),
             pltpu.VMEM((4, 8, 128), F32),
             pltpu.VMEM((BLK, 4, 8, 128), F32),
-            pltpu.SemaphoreType.DMA((3 * CHUNKS + 2,)),
+            pltpu.SemaphoreType.DMA((3 * CHUNKS + 4,)),
             pltpu.SemaphoreType.DMA((7,)),
             pltpu.SemaphoreType.DMA((7,)),
             pltpu.SemaphoreType.DMA((8, 16)),
             pltpu.SemaphoreType.DMA((8, 16)),
         ],
         compiler_params=pltpu.CompilerParams(
-            collective_id=0, has_side_effects=True, vmem_limit_bytes=48 * MIB),
+            collective_id=0, has_side_effects=True, vmem_limit_bytes=54 * MIB),
         name="superelement",
     )(interface_block[0], global_iface[0], start_modes[0], stiff_diag[0], stiff_off[0],
       mass_blocks[0], coupling[0])
-    tile = 512
     modes, reduced, assembled = pl.pallas_call(
         result_kernel,
         out_shape=(jax.ShapeDtypeStruct((ROWS, 256), F32),
                    jax.ShapeDtypeStruct((256, 256), F32),
                    jax.ShapeDtypeStruct((4, 128, 128), F32)),
-        grid=(ROWS // tile,),
-        in_specs=[vm] * 5,
-        out_specs=(pl.BlockSpec((tile, 256), lambda i: (i, 0)), anym, anym),
-        scratch_shapes=[pltpu.SemaphoreType.DMA((2,))],
-        compiler_params=pltpu.CompilerParams(vmem_limit_bytes=12 * MIB),
+        in_specs=[vm] * 3,
+        out_specs=(hbm,) * 3,
+        scratch_shapes=[pltpu.SemaphoreType.DMA((PARTS + 2,))],
+        compiler_params=pltpu.CompilerParams(vmem_limit_bytes=4 * MIB),
         name="result",
-    )(yh, yl, ct, reduced, assembled)
+    )(*results)
     return modes[None], reduced[None], assembled
 
 

time: 105 us -> 92.2 us (0.88)
  Pallas kernels: 103 us -> 91.1 us
  local copies, waits for them, and re-layouts: 1.3 us -> 0 us
    pallas_call x1, Pallas kernels: 97.6 us -> 88.9 us  [local(): pl.pallas_call(kernel, out_shape=(pltpu.VMEM((ROWS, 256), F32), pltpu.VME...]
    pallas_call x1, Pallas kernels: 5.07 us -> 2.26 us  [local(): pl.pallas_call(result_kernel, out_shape=(jax.ShapeDtypeStruct((ROWS, 256)...]
    unnamed x4 -> x0, local copies, waits for them, and re-layouts: 1.3 us -> none
where the time goes in v5:
time: 92.2 us; the launch traced here: 91.9 us
  Pallas kernels  91.1 us (99%)
    pallas_call x1, Pallas kernels, local(): pl.pallas_call(kernel, out_shape=(pltpu.VMEM((ROWS, 256), F32), pltpu.VME...  88.9 us
    pallas_call x1, Pallas kernels, local(): pl.pallas_call(result_kernel, out_shape=(jax.ShapeDtypeStruct((ROWS, 256)...  2.26 us

profile of v5, /device:TPU:1, one launch (start us, length us, event | category | flops | bytes accessed | tf_op | source)
XLA Modules:
  0.0 91.9 jit_solution(1097219398825614651)
XLA Ops:
  0.6 88.9 %superelement.1 = (f32[4096,256]{1,0:T(8,128)S(1)}, f32[256,256]{1,0:T(8,128)S(1)}, f32[4,128,128]{2,1,0:T(8,128)S(1)}) custom-call(s32[32]{0:T(128)} %bitcast.14, s32[16]{0:T(128)} %bitcast.15, f32[4096,256]{1,0:T(8,128)} %bitcast.9, f32[32,128,128]{2,1,0:T(8,128)} %bitcast.10, f32[32,128,128]{2,1,0:T(8,128)} %bitcast.11, f32[32,128,128]{2,1,0:T(8,128)} %bitcast.12, ...), custom_call_target="tpu_custom_call" | custom-call | tf_op jit(solution)/shard_map/superelement/pallas_call | solution.py:416
  89.5 2.3 %result.1 = (f32[4096,256]{1,0:T(8,128)}, f32[256,256]{1,0:T(8,128)}, f32[4,128,128]{2,1,0:T(8,128)}) custom-call(f32[4096,256]{1,0:T(8,128)S(1)} %get-tuple-element.9.refs_0_, f32[256,256]{1,0:T(8,128)S(1)} %get-tuple-element.10.refs_1_, f32[4,128,128]{2,1,0:T(8,128)S(1)} %get-tuple-element.11.refs_2_), custom_call_target="tpu_custom_call" | custom-call | tf_op jit(solution)/shard_map/result/pallas_call | solution.py:456

commit v6 on v5

--- a/solution.py
+++ b/solution.py
@@ -84,7 +84,7 @@
 
 def kernel(ids_hbm, owned_hbm, x_hbm, d_hbm, e_hbm, m_hbm, c_hbm, modes_ref, red_ref, asm_ref,
            ids, owned, x, d, e, m, cpl, xh, xl, fh, fl, yh, yl, ah, al, cum, ct,
-           edge, halo, enext, gram, gram_in, sums, w, w_in, fa, fx,
+           edge, halo, enext, gram, gram_in, sums, w, w_in, fb,
            cond, cond_in, dense, dense_in, slab, slab_in,
            load_sem, halo_send, halo_recv, send_sem, recv_sem):
     me = lax.axis_index("blk")
@@ -319,30 +319,32 @@
     gathered(1)
 
     size = 256
+    column = lax.broadcasted_iota(jnp.int32, (size, size), 1)
     row = lax.broadcasted_iota(jnp.int32, (size, size), 0)
-    column = lax.broadcasted_iota(jnp.int32, (size, size), 1)
     for t in range(2):
         g = sums[t]
-        fa[t] = (g + g.T) * 0.5
-        fx[t] = jnp.where(row == column, 1.0, 0.0)
+        fb[t] = (g + g.T) * 0.5
     for k in range(4):
         lo, hi = 64 * k, 64 * (k + 1)
-        inv = diag_inverse([fa[t, lo:hi, lo:hi] for t in range(2)])
+        inv = diag_inverse([fb[t, lo:hi, lo:hi] for t in range(2)])
+        inside = jnp.logical_and(column >= lo, column < hi)
         for t in range(2):
-            tri = inv[t][:, 64:]
-            xu = mmh(tri, fx[t, lo:hi, :])
-            fx[t, lo:hi, :] = xu
+            unit = jnp.where(column[:64] == row[:64] + lo, 1.0, 0.0)
+            u = mmh(inv[t][:, 64:], jnp.where(inside[:64], unit, fb[t, lo:hi, :]))
+            fb[t, lo:hi, :] = u
             if k < 3:
-                au = mmh(tri, fa[t, lo:hi, :])
-                low = au[:, hi:].T
-                fa[t, hi:, :] = fa[t, hi:, :] - mmh(low, au)
-                fx[t, hi:, :] = fx[t, hi:, :] - mmh(low, xu)
+                low = u.T[hi:, :]
+                fb[t, hi:, :] = jnp.where(inside[hi:], 0.0, fb[t, hi:, :]) - mmh(low, u)
+    lower = column // 64 <= row // 64
+
+    def inverse_of(t):
+        return jnp.where(lower, fb[t], 0.0)
 
     total = w[me]
     for p in peers:
         copy(w.at[p], w_in.at[p], 4, p, p).wait_recv()
         total = total + w_in[p]
-    scaled = mmh(fx[1], total)
+    scaled = mmh(inverse_of(1), total)
     cond[...] = mmh(scaled.T, scaled)
 
     def eight(p):
@@ -356,9 +358,8 @@
         h, l = yh[own(p), :], yl[own(p), :]
         modes_ref[rows_at(p * 256, 256), :] = mm(cat([h, h, l], 1), ct[...])
 
-    inverse = fx[0]
+    inverse = inverse_of(0)
     turned = inverse.T
-    red_ref[...] = mmh(mmh(inverse, sums[1]), turned)
     h, l = split(turned * 256.0)
     ct[...] = cat([h, l, h], 0)
     pairs(modes, 0, 4)
@@ -386,11 +387,14 @@
     for c in slab_out:
         c.start()
     asm_ref[:, eight(me), :] = acc
+    red_ref[...] = mmh(mmh(inverse, sums[1]), turned)
     pairs(modes, 10, 16)
+    for c in started + w_out + cond_out + dense_out:
+        c.wait_send()
     for p in peers:
         copy(slab, slab_in.at[p], 7, p, p).wait_recv()
         asm_ref[:, eight(p), :] = slab_in[p]
-    for c in started + w_out + cond_out + dense_out + slab_out:
+    for c in slab_out:
         c.wait_send()
 
 
@@ -434,7 +438,6 @@
             pltpu.VMEM((2, 256, 256), F32),
             pltpu.VMEM((BLK, 256, 128), F32),
             pltpu.VMEM((BLK, 256, 128), F32),
-            pltpu.VMEM((2, 256, 256), F32),
             pltpu.VMEM((2, 256, 256), F32),
             pltpu.VMEM((128, 128), F32),
             pltpu.VMEM((BLK, 8, 128), F32),

time: 92.2 us -> 90.9 us (0.986)
  Pallas kernels: 91.1 us -> 89.9 us
    pallas_call x1, Pallas kernels: 88.9 us -> 87.7 us  [local(): pl.pallas_call(kernel, out_shape=(pltpu.VMEM((ROWS, 256), F32), pltpu.VME...]
where the time goes in v6:
time: 90.9 us; the launch traced here: 90.7 us
  Pallas kernels  89.9 us (99%)
    pallas_call x1, Pallas kernels, local(): pl.pallas_call(kernel, out_shape=(pltpu.VMEM((ROWS, 256), F32), pltpu.VME...  87.7 us
    pallas_call x1, Pallas kernels, local(): pl.pallas_call(result_kernel, out_shape=(jax.ShapeDtypeStruct((ROWS, 256)...  2.26 us

profile of v6, /device:TPU:1, one launch (start us, length us, event | category | flops | bytes accessed | tf_op | source)
XLA Modules:
  0.0 90.7 jit_solution(13061289149241568282)
XLA Ops:
  0.6 87.7 %superelement.1 = (f32[4096,256]{1,0:T(8,128)S(1)}, f32[256,256]{1,0:T(8,128)S(1)}, f32[4,128,128]{2,1,0:T(8,128)S(1)}) custom-call(s32[32]{0:T(128)} %bitcast.14, s32[16]{0:T(128)} %bitcast.15, f32[4096,256]{1,0:T(8,128)} %bitcast.9, f32[32,128,128]{2,1,0:T(8,128)} %bitcast.10, f32[32,128,128]{2,1,0:T(8,128)} %bitcast.11, f32[32,128,128]{2,1,0:T(8,128)} %bitcast.12, ...), custom_call_target="tpu_custom_call" | custom-call | tf_op jit(solution)/shard_map/superelement/pallas_call | solution.py:420
  88.3 2.3 %result.1 = (f32[4096,256]{1,0:T(8,128)}, f32[256,256]{1,0:T(8,128)}, f32[4,128,128]{2,1,0:T(8,128)}) custom-call(f32[4096,256]{1,0:T(8,128)S(1)} %get-tuple-element.9.refs_0_, f32[256,256]{1,0:T(8,128)S(1)} %get-tuple-element.10.refs_1_, f32[4,128,128]{2,1,0:T(8,128)S(1)} %get-tuple-element.11.refs_2_), custom_call_target="tpu_custom_call" | custom-call | tf_op jit(solution)/shard_map/result/pallas_call | solution.py:459
